TPU v7x, 32 devices: a whole 2x2x4 slice. The times are simulated.
32 devices in a mesh: dp: 8 (over y, x, core), tensor: 4 (over z).
Axes of the slice: x: 2, y: 2, z: 4, core: 2. Of those that a mesh axis runs over, the one named last changes fastest.
Arguments:
- inputs: bfloat16 [2, 8, 256, 2048], P(None, 'dp'), may hold values from -6 to 6
- lengths: int32 [2, 8], P(None, 'dp'), may hold values from 64 to 256, as said below
- prompt_mask: int32 [2, 8, 256], P(None, 'dp'), may hold values from 0 to 1, as said below
- partner: int32 [2, 8], P(None, 'dp'), may hold values from 0 to 7, as said below
- positions: int32 [2, 8, 256], P(None, 'dp'), may hold values from 0 to 383, as said below
- attn_gain: bfloat16 [2048], replicated, may hold values from 0.099609375 to 1.8984375
- mlp_gain: bfloat16 [2048], replicated, may hold values from 0.099609375 to 1.8984375
- attention_input_frozen: bfloat16 [2048, 3, 2048], P(None, None, 'tensor'), may hold values from -0.125 to 0.125
- attention_input_first: float32 [3, 2048, 16], replicated, may hold values from -0.125 to 0.125
- attention_input_second: float32 [3, 16, 2048], P(None, None, 'tensor'), may hold values from -0.6 to 0.6
- attention_input_magnitude: float32 [3, 2048], P(None, 'tensor'), may hold values from 0.7 to 1.5
- attention_output_frozen: bfloat16 [2048, 2048], P('tensor'), may hold values from -0.125 to 0.125
- attention_output_first: float32 [2048, 16], P('tensor'), may hold values from -0.125 to 0.125
- attention_output_second: float32 [16, 2048], replicated, may hold values from -0.6 to 0.6
- attention_output_magnitude: float32 [2048], replicated, may hold values from 4 to 16
- feedforward_input_frozen: bfloat16 [2048, 2, 5632], P(None, None, 'tensor'), may hold values from -0.125 to 0.125
- feedforward_input_first: float32 [2, 2048, 16], replicated, may hold values from -0.125 to 0.125
- feedforward_input_second: float32 [2, 16, 5632], P(None, None, 'tensor'), may hold values from -0.6 to 0.6
- feedforward_input_magnitude: float32 [2, 5632], P(None, 'tensor'), may hold values from 0.7 to 1.5
- feedforward_output_frozen: bfloat16 [5632, 2048], P('tensor'), may hold values from -0.078125 to 0.078125
- feedforward_output_first: float32 [5632, 16], P('tensor'), may hold values from -0.078125 to 0.078125
- feedforward_output_second: float32 [16, 2048], replicated, may hold values from -0.6 to 0.6
- feedforward_output_magnitude: float32 [2048], replicated, may hold values from 1 to 2.5
- grad_out: bfloat16 [2, 8, 256, 2048], P(None, 'dp'), may hold values from -6 to 6
Outputs:
- output: bfloat16 [2, 8, 256, 2048], P(None, 'dp')
- grad_in: bfloat16 [2, 8, 256, 2048], P(None, 'dp')
- attn_in_a_grad: float32 [3, 2048, 16], replicated
- attn_in_b_grad: float32 [3, 16, 2048], P(None, None, 'tensor')
- attn_in_mag_grad: float32 [3, 2048], P(None, 'tensor')
- attn_out_a_grad: float32 [2048, 16], P('tensor')
- attn_out_b_grad: float32 [16, 2048], replicated
- attn_out_mag_grad: float32 [2048], replicated
- mlp_in_a_grad: float32 [2, 2048, 16], replicated
- mlp_in_b_grad: float32 [2, 16, 5632], P(None, None, 'tensor')
- mlp_in_mag_grad: float32 [2, 5632], P(None, 'tensor')
- mlp_out_a_grad: float32 [5632, 16], P('tensor')
- mlp_out_b_grad: float32 [16, 2048], replicated
- mlp_out_mag_grad: float32 [2048], replicated
Inputs may be any that keep to these rules, and one draw needn't show every extreme that they name: `lengths`: in every micro-batch the rows form pairs (partner of partner is the row itself): a prompt row holds the pair's prompt and then the chosen response, its partner, a response row, holds the rejected response alone. Valid tokens fill a row's first slots. `prompt_mask`: 1 exactly on the first slots of a prompt row that hold its prompt, at most 128 of them; 0 everywhere in a response row. `partner`: the other row of the row's pair, in the same micro-batch. `positions`: in a prompt row the slot's index; in a response row the slot's index plus the prompt length of its partner.
All inputs are finite; a program needn't handle non-finite values.
Results may differ from a plain program's by a relative error of at most 0.028.
Values may be sent and summed in bfloat16 or wider, within the bound.
No kernel may reach another device: no remote copies, remote signals or barrier semaphores. Data moves between devices by JAX's collectives and lax.ppermute only.
A program may use at most 384 MiB of HBM per device.

v0:
```python
import math

import jax
import jax.numpy as jnp
from jax import lax
from jax.sharding import PartitionSpec as P

HEAD_DIM = 128
ADAPTER_RANK = 16
ADAPTER_NUMER = 32


epsilon = 1e-05
rope_base = 10000.0
highest_precision = lax.Precision.HIGHEST
masked_score = -1e30


def rms_scale(values):
    return lax.rsqrt(jnp.mean(values * values, axis=-1, keepdims=True) + epsilon)


def rms_back(values, scale_rows, gain_row, gradient):
    scaled_update = gradient * gain_row
    normal = values * scale_rows
    return scale_rows * (
        scaled_update - normal * jnp.mean(scaled_update * normal, axis=-1, keepdims=True)
    )


def turn_half(values):
    middle = values.shape[-1] // 2
    return jnp.concatenate([-values[..., middle:], values[..., :middle]], axis=-1)


def rope_tables(positions, head_size):
    indices = jnp.arange(head_size // 2, dtype=jnp.float32)
    inverse = rope_base ** (-2.0 * indices / head_size)
    angles = positions.astype(jnp.float32)[:, None] * inverse[None, :]
    angles = jnp.concatenate([angles, angles], axis=-1)
    return (jnp.cos(angles)[:, None, :], jnp.sin(angles)[:, None, :])


def contract_rows(left_factor, right_factor):
    return lax.dot_general(
        left_factor, right_factor, (((0,), (0,)), ((), ())), preferred_element_type=jnp.float32
    )


def contract_cols(left_factor, right_factor):
    return lax.dot_general(
        left_factor, right_factor, (((1,), (1,)), ((), ())), preferred_element_type=jnp.float32
    )


def pick_partner(partner_row, far_slots, current, pieces):
    piece_rows = pieces[0].shape[0]
    wanted = partner_row * far_slots + jnp.arange(far_slots, dtype=jnp.int32)
    inside = (wanted >= 0) & (wanted < piece_rows)
    clipped = jnp.clip(wanted, 0, piece_rows - 1)
    packed = jnp.where(inside[:, None], jnp.take(pieces[0], clipped, axis=0), current[0])
    flags = jnp.where(inside, jnp.take(pieces[1], clipped, axis=0), current[1])
    return (packed, flags)


def place_far(partner_row, far_grad, row_count):
    far_slots = far_grad.shape[0]
    owners = jnp.arange(row_count // far_slots, dtype=jnp.int32)
    term = jnp.where((owners == partner_row)[:, None, None], far_grad[None], 0.0)
    return term.reshape(row_count, far_grad.shape[1])


def column_gradient_list(
    weight_total,
    merged_matrix,
    column_norm_value,
    column_magnitude,
    left_factor,
    right_factor,
    adapter_scale,
):
    inner = jnp.sum(weight_total * merged_matrix, axis=0)
    merged_matrix_gradient = (
        column_magnitude
        / column_norm_value
        * (weight_total - inner / (column_norm_value * column_norm_value) * merged_matrix)
    )
    left_factor_gradient = adapter_scale * jnp.einsum(
        "ypz,pvz->pyv", merged_matrix_gradient, right_factor, precision=highest_precision
    )
    right_factor_gradient = adapter_scale * jnp.einsum(
        "emn,mez->enz", left_factor, merged_matrix_gradient, precision=highest_precision
    )
    return (left_factor_gradient, right_factor_gradient, inner / column_norm_value)


def row_pieces_list(
    weight_total,
    merged_matrix,
    column_norm_value,
    column_magnitude,
    left_factor,
    right_factor,
    adapter_scale,
):
    scaled_update = weight_total * (column_magnitude / column_norm_value)
    inner = jnp.sum(weight_total * merged_matrix, axis=0)
    left_factor_part = adapter_scale * jnp.dot(
        scaled_update, right_factor.T, precision=highest_precision
    )
    right_factor_part = adapter_scale * jnp.dot(
        left_factor.T, scaled_update, precision=highest_precision
    )
    return (inner, left_factor_part, right_factor_part)


def on_device(
    inputs,
    lengths,
    prompt_mask,
    partner,
    positions,
    attn_gain,
    mlp_gain,
    attention_input_frozen,
    attention_input_first,
    attention_input_second,
    attention_input_magnitude,
    attention_output_frozen,
    attention_output_first,
    attention_output_second,
    attention_output_magnitude,
    feedforward_input_frozen,
    feedforward_input_first,
    feedforward_input_second,
    feedforward_input_magnitude,
    feedforward_output_frozen,
    feedforward_output_first,
    feedforward_output_second,
    feedforward_output_magnitude,
    grad_out,
):
    micro_count = inputs.shape[0]
    slot_count = inputs.shape[2]
    model_width = inputs.shape[3]
    head_cols = attention_input_frozen.shape[2]
    head_count = head_cols // HEAD_DIM
    unit_count = feedforward_input_frozen.shape[2]
    adapter_scale = ADAPTER_NUMER / ADAPTER_RANK
    score_scale = 1.0 / math.sqrt(HEAD_DIM)
    block_rows = min(512, slot_count)
    block_count = slot_count // block_rows
    attn_scale = attn_gain.astype(jnp.float32)
    mlp_scale = mlp_gain.astype(jnp.float32)
    query_key_value_merged = attention_input_frozen.astype(
        jnp.float32
    ) + adapter_scale * jnp.einsum(
        "kdr,kro->dko", attention_input_first, attention_input_second, precision=highest_precision
    )
    query_key_value_norm = jnp.sqrt(
        jnp.sum(query_key_value_merged * query_key_value_merged, axis=0)
    )
    qkv_weight = (
        (query_key_value_merged * (attention_input_magnitude / query_key_value_norm))
        .astype(jnp.bfloat16)
        .reshape(model_width, 3 * head_cols)
    )
    gate_merged_weight = feedforward_input_frozen.astype(jnp.float32) + adapter_scale * jnp.einsum(
        "kdr,kro->dko",
        feedforward_input_first,
        feedforward_input_second,
        precision=highest_precision,
    )
    gate_column_norm = jnp.sqrt(jnp.sum(gate_merged_weight * gate_merged_weight, axis=0))
    gate_up_weight = (
        (gate_merged_weight * (feedforward_input_magnitude / gate_column_norm))
        .astype(jnp.bfloat16)
        .reshape(model_width, 2 * unit_count)
    )
    output_merged_weight = attention_output_frozen.astype(jnp.float32) + adapter_scale * jnp.dot(
        attention_output_first, attention_output_second, precision=highest_precision
    )
    down_merged_weight = feedforward_output_frozen.astype(jnp.float32) + adapter_scale * jnp.dot(
        feedforward_output_first, feedforward_output_second, precision=highest_precision
    )
    out_square = jnp.sum(output_merged_weight * output_merged_weight, axis=0)
    down_square = jnp.sum(down_merged_weight * down_merged_weight, axis=0)
    output_cross_term = jnp.dot(
        attention_output_first.T, output_merged_weight, precision=highest_precision
    )
    down_cross_term = jnp.dot(
        feedforward_output_first.T, down_merged_weight, precision=highest_precision
    )
    out_square, down_square, output_cross_term, down_cross_term = (
        lax.psum(out_square.astype(jnp.bfloat16), "tensor").astype(jnp.float32),
        lax.psum(down_square.astype(jnp.bfloat16), "tensor").astype(jnp.float32),
        lax.psum(output_cross_term.astype(jnp.bfloat16), "tensor").astype(jnp.float32),
        lax.psum(down_cross_term.astype(jnp.bfloat16), "tensor").astype(jnp.float32),
    )
    output_column_norm = jnp.sqrt(out_square)
    down_column_norm = jnp.sqrt(down_square)
    out_weight = (output_merged_weight * (attention_output_magnitude / output_column_norm)).astype(
        jnp.bfloat16
    )
    down_weight = (down_merged_weight * (feedforward_output_magnitude / down_column_norm)).astype(
        jnp.bfloat16
    )
    grad_qkv = jnp.zeros((model_width, 3 * head_cols), jnp.float32)
    output_projection_gradient = jnp.zeros((head_cols, model_width), jnp.float32)
    grad_gate_up = jnp.zeros((model_width, 2 * unit_count), jnp.float32)
    down_projection_gradient = jnp.zeros((unit_count, model_width), jnp.float32)
    results = []
    input_grads = []
    for micro_at in range(micro_count):
        tokens = inputs[micro_at, 0].astype(jnp.float32)
        length_now = lengths[micro_at, 0]
        partner_row = partner[micro_at, 0]
        cosine, sine_tab = rope_tables(positions[micro_at, 0], HEAD_DIM)
        live_mask = (jnp.arange(slot_count) < length_now).astype(jnp.float32)[:, None]
        attn_rows = rms_scale(tokens)
        normed = (tokens * attn_rows * attn_scale).astype(jnp.bfloat16)
        projected = jnp.dot(normed, qkv_weight, preferred_element_type=jnp.float32).reshape(
            slot_count, 3, head_count, HEAD_DIM
        )
        queries = (projected[:, 0] * cosine + turn_half(projected[:, 0]) * sine_tab).astype(
            jnp.bfloat16
        )
        keys_rot = (projected[:, 1] * cosine + turn_half(projected[:, 1]) * sine_tab).astype(
            jnp.bfloat16
        )
        values_in = projected[:, 2].astype(jnp.bfloat16)
        own_pack = jnp.concatenate(
            [keys_rot.reshape(slot_count, head_cols), values_in.reshape(slot_count, head_cols)],
            axis=1,
        )
        own_flags = prompt_mask[micro_at, 0].astype(jnp.bfloat16)
        empty_pack = (
            jnp.zeros((slot_count, 2 * head_cols), jnp.bfloat16),
            jnp.zeros((slot_count,), jnp.bfloat16),
        )
        far_pack, far_flags = pick_partner(
            partner_row,
            slot_count,
            empty_pack,
            (
                lax.all_gather(own_pack, "dp", axis=0, tiled=True),
                lax.all_gather(own_flags, "dp", axis=0, tiled=True),
            ),
        )
        all_keys = jnp.concatenate(
            [keys_rot, far_pack[:, :head_cols].reshape(slot_count, head_count, HEAD_DIM)], axis=0
        )
        all_values = jnp.concatenate(
            [values_in, far_pack[:, head_cols:].reshape(slot_count, head_count, HEAD_DIM)], axis=0
        )
        far_ok = far_flags > 0

        def block_scores(queries_blk, first_row):
            raw = (
                jnp.einsum(
                    "ihd,jhd->hij", queries_blk, all_keys, preferred_element_type=jnp.float32
                )
                * score_scale
            )
            rows_at = first_row + jnp.arange(block_rows)[:, None]
            own_ok = jnp.arange(slot_count)[None, :] <= rows_at
            allowed = jnp.concatenate(
                [own_ok, jnp.broadcast_to(far_ok[None, :], (block_rows, slot_count))], axis=1
            )
            return jnp.where(allowed[None], raw, masked_score)

        def forward_block(block_at):
            first_row = block_at * block_rows
            scores = block_scores(queries, first_row)
            row_top = jnp.max(scores, axis=-1, keepdims=True)
            exponent = jnp.exp(scores - row_top)
            row_total = jnp.sum(exponent, axis=-1, keepdims=True)
            shares = (exponent / row_total).astype(jnp.bfloat16)
            attended_blk = jnp.einsum(
                "hij,jhd->ihd", shares, all_values, preferred_element_type=jnp.float32
            )
            return (
                attended_blk.reshape(block_rows, head_cols).astype(jnp.bfloat16),
                row_top,
                row_total,
            )

        attended, row_tops, row_totals = lax.map(
            forward_block, jnp.arange(block_count, dtype=jnp.int32)
        )
        attended = attended.reshape(slot_count, head_cols)
        branch = lax.psum(
            jnp.dot(attended, out_weight, preferred_element_type=jnp.float32).astype(jnp.bfloat16),
            "tensor",
        ).astype(jnp.float32)
        middle = tokens + live_mask * branch
        mlp_rows = rms_scale(middle)
        normed_mlp = (middle * mlp_rows * mlp_scale).astype(jnp.bfloat16)
        gate_up = jnp.dot(normed_mlp, gate_up_weight, preferred_element_type=jnp.float32)
        gate_pre = gate_up[:, :unit_count]
        up_pre = gate_up[:, unit_count:]
        gate_sigmoid = jax.nn.sigmoid(gate_pre)
        activated = gate_pre * gate_sigmoid
        hidden = (activated * up_pre).astype(jnp.bfloat16)
        branch_mlp = lax.psum(
            jnp.dot(hidden, down_weight, preferred_element_type=jnp.float32).astype(jnp.bfloat16),
            "tensor",
        ).astype(jnp.float32)
        results.append((middle + live_mask * branch_mlp).astype(jnp.bfloat16))
        upstream = grad_out[micro_at, 0].astype(jnp.float32)
        down_grad = (live_mask * upstream).astype(jnp.bfloat16)
        hidden_grad = contract_cols(down_grad, down_weight)
        down_projection_gradient = down_projection_gradient + contract_rows(hidden, down_grad)
        gate_grad = (
            hidden_grad * up_pre * gate_sigmoid * (1.0 + gate_pre * (1.0 - gate_sigmoid))
        ).astype(jnp.bfloat16)
        up_grad = (hidden_grad * activated).astype(jnp.bfloat16)
        gate_up_grad = jnp.concatenate([gate_grad, up_grad], axis=1)
        grad_gate_up = grad_gate_up + contract_rows(normed_mlp, gate_up_grad)
        mlp_in_grad = lax.psum(
            contract_cols(gate_up_grad, gate_up_weight).astype(jnp.bfloat16), "tensor"
        ).astype(jnp.float32)
        middle_grad = upstream + rms_back(middle, mlp_rows, mlp_scale, mlp_in_grad)
        attn_grad = (live_mask * middle_grad).astype(jnp.bfloat16)
        output_projection_gradient = output_projection_gradient + contract_rows(attended, attn_grad)
        attended_grad = (
            contract_cols(attn_grad, out_weight)
            .astype(jnp.bfloat16)
            .reshape(slot_count, head_count, HEAD_DIM)
        )

        def backward_block(carried, block_at):
            first_row = block_at * block_rows
            row_top = row_tops[block_at]
            row_total = row_totals[block_at]
            scores = block_scores(queries, first_row)
            shares = jnp.exp(scores - row_top) / row_total
            shares_low = shares.astype(jnp.bfloat16)
            share_grad = jnp.einsum(
                "ihd,jhd->hij", attended_grad, all_values, preferred_element_type=jnp.float32
            )
            inner = jnp.sum(shares * share_grad, axis=-1, keepdims=True)
            score_grad = (shares * (share_grad - inner)).astype(jnp.bfloat16)
            query_grad = (
                jnp.einsum("hij,jhd->ihd", score_grad, all_keys, preferred_element_type=jnp.float32)
                * score_scale
            )
            key_part = (
                jnp.einsum("hij,ihd->jhd", score_grad, queries, preferred_element_type=jnp.float32)
                * score_scale
            )
            value_part = jnp.einsum(
                "hij,ihd->jhd", shares_low, attended_grad, preferred_element_type=jnp.float32
            )
            query_grad, key_part, value_part = (query_grad, key_part, value_part)
            return ((carried[0] + key_part, carried[1] + value_part), query_grad)

        key_zero = jnp.zeros((slot_count + slot_count, head_count, HEAD_DIM), jnp.float32)
        (key_grad, value_grad), query_grads = lax.scan(
            backward_block, (key_zero, key_zero), jnp.arange(block_count, dtype=jnp.int32)
        )
        far_grad = jnp.concatenate(
            [
                key_grad[slot_count:].reshape(slot_count, head_cols),
                value_grad[slot_count:].reshape(slot_count, head_cols),
            ],
            axis=1,
        )
        far_low = far_grad.astype(jnp.bfloat16)
        returned = lax.psum_scatter(
            place_far(
                partner_row, far_low.astype(jnp.float32), slot_count * lax.axis_size("dp")
            ).astype(jnp.bfloat16),
            "dp",
            scatter_dimension=0,
            tiled=True,
        ).astype(jnp.float32)
        key_total = key_grad[:slot_count] + returned[:, :head_cols].reshape(
            slot_count, head_count, HEAD_DIM
        )
        value_total = value_grad[:slot_count] + returned[:, head_cols:].reshape(
            slot_count, head_count, HEAD_DIM
        )
        query_total = query_grads.reshape(slot_count, head_count, HEAD_DIM)
        query_back = (query_total * cosine - turn_half(query_total * sine_tab)).astype(jnp.bfloat16)
        key_back = (key_total * cosine - turn_half(key_total * sine_tab)).astype(jnp.bfloat16)
        value_back = value_total.astype(jnp.bfloat16)
        qkv_grad = jnp.concatenate(
            [
                query_back.reshape(slot_count, head_cols),
                key_back.reshape(slot_count, head_cols),
                value_back.reshape(slot_count, head_cols),
            ],
            axis=1,
        )
        grad_qkv = grad_qkv + contract_rows(normed, qkv_grad)
        attn_in_grad = lax.psum(
            contract_cols(qkv_grad, qkv_weight).astype(jnp.bfloat16), "tensor"
        ).astype(jnp.float32)
        input_grads.append(
            (middle_grad + rms_back(tokens, attn_rows, attn_scale, attn_in_grad)).astype(
                jnp.bfloat16
            )
        )
    query_key_value_total = grad_qkv.reshape(model_width, 3, head_cols)
    gate_weight_total = grad_gate_up.reshape(model_width, 2, unit_count)
    qkv_left, qkv_right, qkv_mag = column_gradient_list(
        query_key_value_total,
        query_key_value_merged,
        query_key_value_norm,
        attention_input_magnitude,
        attention_input_first,
        attention_input_second,
        adapter_scale,
    )
    gate_left, gate_right, gate_mag = column_gradient_list(
        gate_weight_total,
        gate_merged_weight,
        gate_column_norm,
        feedforward_input_magnitude,
        feedforward_input_first,
        feedforward_input_second,
        adapter_scale,
    )
    out_inner, output_left_factor, output_right_factor = row_pieces_list(
        output_projection_gradient,
        output_merged_weight,
        output_column_norm,
        attention_output_magnitude,
        attention_output_first,
        attention_output_second,
        adapter_scale,
    )
    down_inner, down_left_factor, down_right_factor = row_pieces_list(
        down_projection_gradient,
        down_merged_weight,
        down_column_norm,
        feedforward_output_magnitude,
        feedforward_output_first,
        feedforward_output_second,
        adapter_scale,
    )
    qkv_left, gate_left, output_right_factor, down_right_factor, out_inner, down_inner = lax.psum(
        (qkv_left, gate_left, output_right_factor, down_right_factor, out_inner, down_inner),
        ("dp", "tensor"),
    )
    qkv_right, qkv_mag, gate_right, gate_mag, output_left_factor, down_left_factor = (
        lax.psum(qkv_right.astype(jnp.bfloat16), "dp").astype(jnp.float32),
        lax.psum(qkv_mag.astype(jnp.bfloat16), "dp").astype(jnp.float32),
        lax.psum(gate_right.astype(jnp.bfloat16), "dp").astype(jnp.float32),
        lax.psum(gate_mag.astype(jnp.bfloat16), "dp").astype(jnp.float32),
        lax.psum(output_left_factor.astype(jnp.bfloat16), "dp").astype(jnp.float32),
        lax.psum(down_left_factor.astype(jnp.bfloat16), "dp").astype(jnp.float32),
    )
    output_norm_factor = (
        attention_output_magnitude
        * out_inner
        / (output_column_norm * output_column_norm * output_column_norm)
    )
    down_norm_factor = (
        feedforward_output_magnitude
        * down_inner
        / (down_column_norm * down_column_norm * down_column_norm)
    )
    output_left_factor = output_left_factor - adapter_scale * jnp.dot(
        output_merged_weight * output_norm_factor,
        attention_output_second.T,
        precision=highest_precision,
    )
    down_left_factor = down_left_factor - adapter_scale * jnp.dot(
        down_merged_weight * down_norm_factor,
        feedforward_output_second.T,
        precision=highest_precision,
    )
    output_right_factor = (
        output_right_factor - adapter_scale * output_cross_term * output_norm_factor
    )
    down_right_factor = down_right_factor - adapter_scale * down_cross_term * down_norm_factor
    out_mag = out_inner / output_column_norm
    down_mag = down_inner / down_column_norm
    layer_out = jnp.stack(results)[:, None]
    layer_grad = jnp.stack(input_grads)[:, None]
    return (
        layer_out,
        layer_grad,
        qkv_left,
        qkv_right,
        qkv_mag,
        output_left_factor,
        output_right_factor,
        out_mag,
        gate_left,
        gate_right,
        gate_mag,
        down_left_factor,
        down_right_factor,
        down_mag,
    )


def solution(mesh):
    in_specs = (
        P(None, "dp", None, None),
        P(None, "dp"),
        P(None, "dp", None),
        P(None, "dp"),
        P(None, "dp", None),
        P(),
        P(),
        P(None, None, "tensor"),
        P(),
        P(None, None, "tensor"),
        P(None, "tensor"),
        P("tensor", None),
        P("tensor", None),
        P(),
        P(),
        P(None, None, "tensor"),
        P(),
        P(None, None, "tensor"),
        P(None, "tensor"),
        P("tensor", None),
        P("tensor", None),
        P(),
        P(),
        P(None, "dp", None, None),
    )
    out_specs = (
        P(None, "dp", None, None),
        P(None, "dp", None, None),
        P(),
        P(None, None, "tensor"),
        P(None, "tensor"),
        P("tensor", None),
        P(),
        P(),
        P(),
        P(None, None, "tensor"),
        P(None, "tensor"),
        P("tensor", None),
        P(),
        P(),
    )
    return jax.shard_map(
        on_device, mesh=mesh, in_specs=in_specs, out_specs=out_specs, check_vma=False
    )
```

profile of v0, /device:TPU:0, one launch (start us, length us, event | category | flops | bytes accessed | tf_op | source)
XLA Modules:
  0.0 1090.8 jit_solution(10343080176123279099)
XLA Ops:
  9.3 9.0 copy.69
  18.3 15.6 %multiply_reduce_fusion.3 = (f32[3,512]{1,0:T(4,128)S(1)}, f32[2048,3,512]{0,2,1:T(8,128)}) fusion(f32[3,16,512]{2,1,0:T(8,128)S(1)} %copy-done.101, f32[3,2048,16]{1,2,0:T(8,128)S(1)} %copy-done, bf16[2048,3,512]{0,2,1:T(8,128)(2,1)} %copy.69), kind=kOutput, calls=%fused_computation.15 | convolution fusion | flops 619706880 | bytes 19372032 | tf_op jit(solution)/shard_map/kdr,kro->dko/dot_general | solution.py:157
  33.9 8.0 multiply_convert_fusion.1
  42.0 4.8 fusion.116
  67.6 4.8 fusion.111
  88.8 10.3 all-gather.1
  99.1 8.9 all-gather
  112.1 28.9 %copy.78 = bf16[2048,2,1408]{0,2,1:T(8,128)(2,1)} copy(bf16[2048,2,1408]{2,1,0:T(2,128)(2,1)} %param.43) | data formatting | bytes 23068672 | tf_op args[15]
  141.0 6.8 multiply_reduce_fusion.7
  147.8 12.2 %psum.168 = bf16[2048]{0:T(1024)(128)(2,1)S(1)} all-reduce(bf16[2048]{0:T(1024)(128)(2,1)S(1)} %get-tuple-element.271), channel_id=1, replica_groups=mesh['dp'=8,'tensor'=4] {'tensor'}, use_global_device_ids=true, to_apply=%region_5.8 | all-reduce | flops 2048 | bytes 8192 | tf_op jit(solution)/shard_map/psum | solution.py:195
  166.8 26.1 %multiply_reduce_fusion.1 = (f32[2,1408]{1,0:T(2,128)S(1)}, f32[2048,2,1408]{0,2,1:T(8,128)}) fusion(f32[2,16,1408]{2,1,0:T(8,128)S(1)} %copy-done.84, f32[2,2048,16]{1,2,0:T(8,128)S(1)} %copy-done.63, bf16[2048,2,1408]{0,2,1:T(8,128)(2,1)} %copy.78), kind=kOutput, calls=%fused_computation.10 | convolution fusion | flops 1136129280 | bytes 35056640 | tf_op jit(solution)/shard_map/kdr,kro->dko/dot_general | solution.py:168
  195.4 13.7 %multiply_add_fusion = f32[1408,2048]{1,0:T(8,128)} fusion(bf16[1408,2048]{1,0:T(8,128)(2,1)} %param.47, f32[1408,16]{0,1:T(8,128)S(1)} %copy-done.53, f32[16,2048]{1,0:T(8,128)S(1)} %copy-done.61), kind=kOutput, calls=%fused_computation.21 | convolution fusion | flops 562298880 | bytes 17522688 | tf_op jit(solution)/shard_map/dot_general | solution.py:183
  237.6 13.7 %multiply_convert_fusion = bf16[2048,2,1408]{0,2,1:T(8,128)(2,1)} fusion(f32[2048,2,1408]{0,2,1:T(8,128)} %get-tuple-element.266, f32[2,1408]{1,0:T(2,128)S(1)} %copy-done.97), kind=kLoop, calls=%fused_computation.9 | loop fusion | flops 11534336 | bytes 34614272 | tf_op jit(solution)/shard_map/convert_element_type | solution.py:177
  251.4 70.7 %all-reduce.23.cloned.1.call-done = (bf16[256,2048]{1,0:T(8,128)(2,1)}, bf16[256,2048]{1,0:T(8,128)(2,1)}) async-done(((bf16[256,2048]{1,0:T(8,128)(2,1)}, bf16[256,2048]{1,0:T(8,128)(2,1)}), (bf16[256,2048]{1,0:T(8,128)(2,1)}, bf16[256,2048]{1,0:T(8,128)(2,1)})) %all-reduce.23.cloned.1.call-update) | async-done | bytes 2097168 | tf_op jit(solution)/shard_map/psum | solution.py:292
  324.7 6.4 fusion.203
  333.1 9.4 fusion.202
  345.0 5.9 fusion.157
  350.9 9.0 multiply_reduce_fusion.4
  359.9 10.5 psum.170
  371.7 8.5 multiply_convert_fusion.2
  380.3 5.7 multiply_convert_fusion.11
  402.1 82.5 %all-reduce.21.cloned.1.call-done = (bf16[256,2048]{1,0:T(8,128)(2,1)}, bf16[256,2048]{1,0:T(8,128)(2,1)}) async-done(((bf16[256,2048]{1,0:T(8,128)(2,1)}, bf16[256,2048]{1,0:T(8,128)(2,1)}), (bf16[256,2048]{1,0:T(8,128)(2,1)}, bf16[256,2048]{1,0:T(8,128)(2,1)})) %all-reduce.21.cloned.1.call-update) | async-done | bytes 2097168 | tf_op jit(solution)/shard_map/psum | solution.py:320
  509.3 5.4 fusion.62
  514.7 11.1 %fusion.63 = bf16[16,2048]{1,0:T(8,128)(2,1)} fusion(f32[1408,2048]{1,0:T(8,128)} %multiply_add_fusion, f32[1408,16]{0,1:T(8,128)S(1)} %copy-done.54), kind=kOutput, calls=%fused_computation.93 | convolution fusion | flops 553680896 | bytes 11689984 | tf_op jit(solution)/shard_map/dot_general | solution.py:191
  525.9 9.6 fusion.135
  550.4 15.9 %convolution_add_fusion = f32[2048,2816]{1,0:T(8,128)} fusion(f32[2048,2816]{1,0:T(8,128)} %fusion.135, bf16[256,1408]{1,0:T(8,128)(2,1)} %copy-done.90, bf16[256,1408]{1,0:T(8,128)(2,1)} %copy-done.89, bf16[256,2048]{1,0:T(8,128)(2,1)S(1)} %copy-done.15, f32[256]{0:T(256)} %copy-done.140, f32[256]{0:T(256)S(1)} %get-tuple-element.296, ...), kind=kOutput, calls=%fused_computation.26 | convolution fusion | flops 2965110784 | bytes 49686528 | tf_op jit(solution)/shard_map/dot_general | solution.py:45
  566.3 23.8 %copy.95 = f32[2048,2816]{0,1:T(8,128)} copy(f32[2048,2816]{1,0:T(8,128)} %convolution_add_fusion) | data formatting | bytes 46137344 | tf_op jit(solution)/shard_map/add | solution.py:319
  590.0 15.7 %multiply_reduce_fusion = f32[2,1408]{1,0:T(2,128)S(1)} fusion(f32[2048,2,1408]{0,2,1:T(8,128)} %bitcast.300, f32[2048,2,1408]{0,2,1:T(8,128)} %get-tuple-element.266), kind=kLoop, calls=%fused_computation.8 | loop fusion | flops 11531520 | bytes 46148608 | tf_op jit(solution)/shard_map/reduce_sum | solution.py:82
  606.3 5.6 convolution_convert_fusion.6
  611.9 5.5 convolution_convert_fusion.7
  617.5 13.3 %fusion.59 = bf16[1408,16]{0,1:T(8,128)(2,1)} fusion(f32[16,2048]{1,0:T(8,128)S(1)} %copy-done.62, f32[1408,2048]{1,0:T(8,128)} %get-tuple-element.275, f32[2048]{0:T(1024)S(1)} %copy-done.100), kind=kOutput, calls=%fused_computation.89 | convolution fusion | flops 556576768 | bytes 11718656 | tf_op jit(solution)/shard_map/dot_general | solution.py:108
  630.8 27.1 %fusion.37 = bf16[2,16,1408]{2,1,0:T(8,128)(2,1)} fusion(f32[2,2048,16]{1,2,0:T(8,128)} %param.44, f32[2048,2,1408]{0,2,1:T(8,128)} %bitcast.301, f32[2048,2,1408]{0,2,1:T(8,128)} %get-tuple-element.266, f32[2,1408]{1,0:T(2,128)} %get-tuple-element.250, f32[2,1408]{1,0:T(2,128)S(1)} %copy-done.98), kind=kOutput, calls=%fused_computation.81 | convolution fusion | flops 1124687872 | bytes 46512128 | tf_op jit(solution)/shard_map/emn,mez->enz/dot_general | solution.py:91
  665.8 4.4 fusion.105
  679.8 6.5 fusion.118
  686.4 11.3 %convolution_add_fusion.2 = f32[2048,1536]{0,1:T(8,128)} fusion(f32[2048,1536]{0,1:T(8,128)} %fusion.118, f32[256]{0:T(256)S(1)} %copy-done.144, f32[2048]{0:T(1024)S(1)} %copy-done.114, bf16[256,512]{0,1:T(8,128)(2,1)S(1)} %bitcast.336, bf16[256,512]{0,1:T(8,128)(2,1)S(1)} %bitcast.340, bf16[256,512]{0,1:T(8,128)(2,1)S(1)} %bitcast.345, ...), kind=kOutput, calls=%fused_computation.28 | convolution fusion | flops 1618214912 | bytes 27010048 | tf_op jit(solution)/shard_map/dot_general | solution.py:45
  697.8 6.4 multiply_reduce_fusion.2
  704.8 15.6 %fusion.95 = bf16[3,16,512]{2,1,0:T(8,128)(2,1)} fusion(f32[3,2048,16]{1,2,0:T(8,128)S(1)} %copy-done, f32[2048,3,512]{0,2,1:T(8,128)} %bitcast.306, f32[2048,3,512]{0,2,1:T(8,128)S(1)} %bitcast.304, f32[3,512]{1,0:T(4,128)S(1)} %get-tuple-element.252, f32[3,512]{1,0:T(4,128)S(1)} %copy-done.117), kind=kOutput, calls=%fused_computation.169 | convolution fusion | flops 613466112 | bytes 25620480 | tf_op jit(solution)/shard_map/emn,mez->enz/dot_general | solution.py:91
  723.3 5.9 convolution_convert_fusion.4
  729.3 10.0 fusion.56
  739.2 20.7 %fusion.35 = f32[2,2048,16]{1,2,0:T(8,128)} fusion(f32[2,16,1408]{2,1,0:T(8,128)} %param.45, f32[2048,2,1408]{0,2,1:T(8,128)} %bitcast.302, f32[2048,2,1408]{0,2,1:T(8,128)} %get-tuple-element.266, f32[2,1408]{1,0:T(2,128)} %get-tuple-element.250, f32[2,1408]{1,0:T(2,128)S(1)} %copy-done.98), kind=kOutput, calls=%fused_computation.79 | convolution fusion | flops 1124663296 | bytes 46602240 | tf_op jit(solution)/shard_map/ypz,pvz->pyv/dot_general | solution.py:88
  761.5 42.4 %all-reduce = (f32[2048]{0:T(1024)}, f32[2048]{0:T(1024)S(1)}) all-reduce(f32[2048]{0:T(1024)} %get-tuple-element.284, f32[2048]{0:T(1024)} %get-tuple-element.158), channel_id=1, replica_groups=mesh['dp'=8,'tensor'=4] {'dp','tensor'}, use_global_device_ids=true, to_apply=%region_36.39 | all-reduce | flops 4096 | bytes 32768 | tf_op jit(solution)/shard_map/psum | solution.py:443
  806.6 5.3 fusion.41
  811.9 13.5 %fusion.33 = f32[3,2048,16]{1,2,0:T(8,128)} fusion(f32[3,16,512]{2,1,0:T(8,128)S(1)} %copy-done.102, f32[2048,3,512]{0,2,1:T(8,128)} %bitcast.307, f32[2048,3,512]{0,2,1:T(8,128)} %get-tuple-element.268, f32[3,512]{1,0:T(4,128)S(1)} %copy-done.127, f32[3,512]{1,0:T(4,128)S(1)} %copy-done.118), kind=kOutput, calls=%fused_computation.77 | convolution fusion | flops 613515264 | bytes 25669632 | tf_op jit(solution)/shard_map/ypz,pvz->pyv/dot_general | solution.py:88
  829.6 13.8 %fusion.50 = f32[1408,16]{0,1:T(8,128)} fusion(f32[16,2048]{1,0:T(8,128)} %param.49, f32[1408,2048]{1,0:T(8,128)} %multiply_add_fusion, f32[2048]{0:T(1024)} %get-tuple-element.190, bf16[1408,16]{0,1:T(8,128)(2,1)} %get-tuple-element.178), kind=kOutput, calls=%fused_computation.86 | convolution fusion | flops 556599296 | bytes 11808768 | tf_op jit(solution)/shard_map/dot_general | solution.py:470
  843.4 4.4 fusion.102
  847.8 92.7 %all-reduce.19.cloned.1.call-done = (bf16[256,2048]{1,0:T(8,128)(2,1)}, bf16[256,2048]{1,0:T(8,128)(2,1)}, bf16[256,2048]{1,0:T(8,128)(2,1)}, bf16[256,2048]{1,0...) async-done(((bf16[256,2048]{1,0:T(8,128)(2,1)}, bf16[256,2048]{1,0:T(8,128)(2,1)}, bf16[256,2048]{1,0:T(8,128)(2,1)}, bf16[256,2048]{1,0:T(8,128)(2,1)}, ...) | async-done | bytes 4325392 | tf_op jit(solution)/shard_map/psum | solution.py:305
  943.4 4.8 fusion.120
  951.2 125.6 %all-reduce.15.cloned.1.call-done = (f32[3,2048,16]{1,2,0:T(8,128)}, f32[16,2048]{1,0:T(8,128)}, f32[2,2048,16]{1,2,0:T(8,128)}, f32[16,2048]{1,0:T(8,128)}) async-done(((f32[3,2048,16]{1,2,0:T(8,128)}, f32[16,2048]{1,0:T(8,128)}, f32[2,2048,16]{1,2,0:T(8,128)}, f32[16,2048]{1,0:T(8,128)}), (f32[3,2048,16]{1,2,0:T(8,128)}, f32[16,2048]{1,0:T(8,128)}, f32[2,2048,16]{1,2,0:T(8,128)}, ...) | async-done | bytes 917520 | tf_op jit(solution)/shard_map/psum | solution.py:443
  (528 shorter events, 185.2 us)
Async XLA Ops:
  7.2 11.1 %copy-start = (f32[3,2048,16]{1,2,0:T(8,128)S(1)}, f32[3,2048,16]{1,2,0:T(8,128)}, u32[]{:S(2)}) copy-start(f32[3,2048,16]{1,2,0:T(8,128)} %param.36) | copy-start | bytes 1179652
  7.2 202.0 %all-gather.5.cloned.1.call-start = ((), (), s32[]{:S(2)}) async-start(), calls=%async_computation.2 | async-start | bytes 4718592 | tf_op jit(solution)/shard_map/all_gather | solution.py:246
  9.3 58.3 %copy-start.113 = (f32[2048]{0:T(1024)}, f32[2048]{0:T(1024)S(1)}, u32[]{:S(2)}) copy-start(f32[2048]{0:T(1024)S(1)} %convert_element_type.428) | copy-start | bytes 24580
  18.3 23.7 %copy-start.146 = (f32[256]{0:T(256)}, f32[256]{0:T(256)S(1)}, u32[]{:S(2)}) copy-start(f32[256]{0:T(256)S(1)} %get-tuple-element.287) | copy-start | bytes 3076
  18.3 49.3 %copy-start.143 = (f32[256]{0:T(256)}, f32[256]{0:T(256)S(1)}, u32[]{:S(2)}) copy-start(f32[256]{0:T(256)S(1)} %get-tuple-element.286) | copy-start | bytes 3076
  18.3 15.6 %copy-start.152 = (f32[3,512]{1,0:T(4,128)S(1)}, f32[3,512]{1,0:T(4,128)}, u32[]{:S(2)}) copy-start(f32[3,512]{1,0:T(4,128)} %param.38) | copy-start | bytes 18436
  66.1 148.5 %all-gather.7.cloned.1.call-start = ((), (), s32[]{:S(2)}) async-start(), calls=%async_computation.3 | async-start | bytes 4718592 | tf_op jit(solution)/shard_map/all_gather | solution.py:246
  86.7 235.3 %all-reduce.23.cloned.1.call-start = ((), (), s32[]{:S(2)}) async-start(), calls=%async_computation.11 | async-start | bytes 4194304 | tf_op jit(solution)/shard_map/psum | solution.py:292
  112.1 28.9 %copy-start.55 = (f32[16,2048]{1,0:T(8,128)S(1)}, f32[16,2048]{1,0:T(8,128)}, u32[]{:S(2)}) copy-start(f32[16,2048]{1,0:T(8,128)} %param.41) | copy-start | bytes 393220
  112.1 28.9 %copy-start.103 = (f32[512,16]{0,1:T(8,128)S(1)}, f32[512,16]{0,1:T(8,128)}, u32[]{:S(2)}) copy-start(f32[512,16]{0,1:T(8,128)} %param.40) | copy-start | bytes 98308
  141.0 19.5 %copy-start.160 = (s32[2,1]{0,1:T(1,128)S(1)}, s32[2,1]{0,1:T(1,128)}, u32[]{:S(2)}) copy-start(s32[2,1]{0,1:T(1,128)} %param.29) | copy-start | bytes 28
  141.0 21.4 %copy-start.137 = (f32[2048]{0:T(1024)S(1)}, f32[2048]{0:T(1024)}, u32[]{:S(2)}) copy-start(f32[2048]{0:T(1024)} %param.42) | copy-start | bytes 24580
  141.0 25.8 %copy-start.63 = (f32[2,2048,16]{1,2,0:T(8,128)S(1)}, f32[2,2048,16]{1,2,0:T(8,128)}, u32[]{:S(2)}) copy-start(f32[2,2048,16]{1,2,0:T(8,128)} %param.44) | copy-start | bytes 786436
  141.0 25.8 %copy-start.84 = (f32[2,16,1408]{2,1,0:T(8,128)S(1)}, f32[2,16,1408]{2,1,0:T(8,128)}, u32[]{:S(2)}) copy-start(f32[2,16,1408]{2,1,0:T(8,128)} %param.45) | copy-start | bytes 540676
  162.4 387.9 %copy-start.121 = (f32[256]{0:T(256)}, f32[256]{0:T(256)S(1)}, u32[]{:S(2)}) copy-start(f32[256]{0:T(256)S(1)} %get-tuple-element.296) | copy-start | bytes 3076
  162.5 31.1 %copy-start.119 = (f32[2048]{0:T(1024)}, f32[2048]{0:T(1024)S(1)}, u32[]{:S(2)}) copy-start(f32[2048]{0:T(1024)S(1)} %fusion.170) | copy-start | bytes 24580
  166.8 26.1 %copy-start.149 = (f32[2,1408]{1,0:T(2,128)S(1)}, f32[2,1408]{1,0:T(2,128)}, u32[]{:S(2)}) copy-start(f32[2,1408]{1,0:T(2,128)} %param.46) | copy-start | bytes 33796
  166.8 26.7 %copy-start.2 = (f32[512,2048]{1,0:T(8,128)S(1)}, f32[512,2048]{1,0:T(8,128)}, u32[]{:S(2)}) copy-start(f32[512,2048]{1,0:T(8,128)} %get-tuple-element.272) | copy-start | bytes 12582916
  213.8 15.2 %copy-start.78 = (bf16[256,512]{0,1:T(8,128)(2,1)}, bf16[256,512]{0,1:T(8,128)(2,1)S(1)}, u32[]{:S(2)}) copy-start(bf16[256,512]{0,1:T(8,128)(2,1)S(1)} %copy.75) | copy-start | bytes 786436
  237.6 247.0 %all-reduce.21.cloned.1.call-start = ((), (), s32[]{:S(2)}) async-start(), calls=%async_computation.10 | async-start | bytes 4194304 | tf_op jit(solution)/shard_map/psum | solution.py:320
  333.1 17.9 %slice-start = ((s8[11534336]{0:T(1024)(128)(4,1)}), s8[4194304]{0:T(1024)(128)(4,1)S(1)}, s32[]{:S(2)}) async-start(s8[11534336]{0:T(1024)(128)(4,1)} %bitcast.298), calls=%async_computation.12 | async-start | bytes 8388608
  333.1 17.9 %slice-start.1 = ((s8[11534336]{0:T(1024)(128)(4,1)}), s8[3145728]{0:T(1024)(128)(4,1)S(1)}, s32[]{:S(2)}) async-start(s8[11534336]{0:T(1024)(128)(4,1)} %bitcast.298), calls=%async_computation.13 | async-start | bytes 6291456
  399.0 272.7 %reduce-scatter.3.cloned.1.call-start = ((), (), s32[]{:S(2)}) async-start(), calls=%async_computation.4 | async-start | bytes 4718592 | tf_op jit(solution)/shard_map/reduce_scatter | solution.py:370
  506.7 169.3 %reduce-scatter.5.cloned.1.call-start = ((), (), s32[]{:S(2)}) async-start(), calls=%async_computation.5 | async-start | bytes 4718592 | tf_op jit(solution)/shard_map/reduce_scatter | solution.py:370
  514.7 11.1 %copy-start.88 = (bf16[256,1408]{1,0:T(8,128)(2,1)S(1)}, bf16[256,1408]{1,0:T(8,128)(2,1)}, u32[]{:S(2)}) copy-start(bf16[256,1408]{1,0:T(8,128)(2,1)} %copy-done.87) | copy-start | bytes 2162692
  514.7 11.1 %copy-start.134 = (f32[256]{0:T(256)S(1)}, f32[256]{0:T(256)}, u32[]{:S(2)}) copy-start(f32[256]{0:T(256)} %copy-done.132) | copy-start | bytes 3076
  550.3 209.7 %all-reduce.13.cloned.1.call-start = ((), (), s32[]{:S(2)}) async-start(), calls=%async_computation.6 | async-start | bytes 180224 | tf_op jit(solution)/shard_map/psum | solution.py:450
  590.0 15.7 %copy-start.125 = (f32[2,1408]{1,0:T(2,128)S(1)}, f32[2,1408]{1,0:T(2,128)}, u32[]{:S(2)}) copy-start(f32[2,1408]{1,0:T(2,128)} %copy-done.124) | copy-start | bytes 33796
  590.0 16.3 %copy-start.44 = (bf16[256,1408]{1,0:T(8,128)(2,1)S(1)}, bf16[256,1408]{1,0:T(8,128)(2,1)}, u32[]{:S(2)}) copy-start(bf16[256,1408]{1,0:T(8,128)(2,1)} %multiply_convert_fusion.14) | copy-start | bytes 2162692
  617.5 13.3 %copy-start.98 = (f32[2,1408]{1,0:T(2,128)S(1)}, f32[2,1408]{1,0:T(2,128)}, u32[]{:S(2)}) copy-start(f32[2,1408]{1,0:T(2,128)} %sqrt_divide_fusion.1) | copy-start | bytes 33796
  657.9 167.6 %all-reduce.17.cloned.1.call-start = ((), (), s32[]{:S(2)}) async-start(), calls=%async_computation.8 | async-start | bytes 240640 | tf_op jit(solution)/shard_map/psum | solution.py:448
  679.8 17.9 %slice-start.3 = ((s8[12582912]{0:T(1024)(128)(4,1)}), s8[4194304]{0:T(1024)(128)(4,1)S(1)}, s32[]{:S(2)}) async-start(s8[12582912]{0:T(1024)(128)(4,1)} %bitcast.303), calls=%async_computation.15 | async-start | bytes 8388608
  686.3 11.4 %slice-start.4 = ((s8[12582912]{0:T(1024)(128)(4,1)}), s8[4194304]{0:T(1024)(128)(4,1)S(1)}, s32[]{:S(2)}) async-start(s8[12582912]{0:T(1024)(128)(4,1)} %bitcast.303), calls=%async_computation.16 | async-start | bytes 8388608
  686.4 11.4 %slice-start.5 = ((s8[12582912]{0:T(1024)(128)(4,1)}), s8[4194304]{0:T(1024)(128)(4,1)S(1)}, s32[]{:S(2)}) async-start(s8[12582912]{0:T(1024)(128)(4,1)} %bitcast.303), calls=%async_computation.17 | async-start | bytes 8388608
  697.7 22.7 %slice-start.9 = ((s8[6291456]{0:T(1024)(128)(4,1)}), s8[4194304]{0:T(1024)(128)(4,1)S(1)}, s32[]{:S(2)}) async-start(s8[6291456]{0:T(1024)(128)(4,1)} %bitcast.321), calls=%async_computation.21 | async-start | bytes 8388608
  704.8 15.6 %copy-start.126 = (f32[3,512]{1,0:T(4,128)}, f32[3,512]{1,0:T(4,128)S(1)}, u32[]{:S(2)}) copy-start(f32[3,512]{1,0:T(4,128)S(1)} %get-tuple-element.252) | copy-start | bytes 18436
  704.8 15.6 %slice-start.10 = ((s8[6291456]{0:T(1024)(128)(4,1)}), s8[2097152]{0:T(1024)(128)(4,1)S(1)}, s32[]{:S(2)}) async-start(s8[6291456]{0:T(1024)(128)(4,1)} %bitcast.321), calls=%async_computation.22 | async-start | bytes 4194304
  723.3 217.2 %all-reduce.19.cloned.1.call-start = ((), (), s32[]{:S(2)}) async-start(), calls=%async_computation.9 | async-start | bytes 8650752 | tf_op jit(solution)/shard_map/psum | solution.py:305
  729.2 347.6 %all-reduce.15.cloned.1.call-start = ((), (), s32[]{:S(2)}) async-start(), calls=%async_computation.7 | async-start | bytes 1835008 | tf_op jit(solution)/shard_map/psum | solution.py:443
  829.6 13.8 %copy-start.4 = (f32[512,2048]{1,0:T(8,128)S(1)}, f32[512,2048]{1,0:T(8,128)}, u32[]{:S(2)}) copy-start(f32[512,2048]{1,0:T(8,128)} %get-tuple-element.272) | copy-start | bytes 12582916
  829.6 13.8 %copy-start.57 = (f32[16,2048]{1,0:T(8,128)S(1)}, f32[16,2048]{1,0:T(8,128)}, u32[]{:S(2)}) copy-start(f32[16,2048]{1,0:T(8,128)} %param.41) | copy-start | bytes 393220
  829.6 13.8 %copy-start.136 = (f32[2048]{0:T(1024)S(1)}, f32[2048]{0:T(1024)}, u32[]{:S(2)}) copy-start(f32[2048]{0:T(1024)} %get-tuple-element.192) | copy-start | bytes 24580
  829.6 13.8 %copy-start.142 = (bf16[512,16]{0,1:T(8,128)(2,1)S(1)}, bf16[512,16]{0,1:T(8,128)(2,1)}, u32[]{:S(2)}) copy-start(bf16[512,16]{0,1:T(8,128)(2,1)} %get-tuple-element.176) | copy-start | bytes 49156
  843.4 97.1 %copy-start.115 = (f32[2048]{0:T(1024)S(1)}, f32[2048]{0:T(1024)}, u32[]{:S(2)}) copy-start(f32[2048]{0:T(1024)} %copy-done.113) | copy-start | bytes 24580
  949.7 127.2 %copy-start.131 = (bf16[16,2048]{1,0:T(8,128)(2,1)S(1)}, bf16[16,2048]{1,0:T(8,128)(2,1)}, u32[]{:S(2)}) copy-start(bf16[16,2048]{1,0:T(8,128)(2,1)} %get-tuple-element.183) | copy-start | bytes 196612
  949.7 127.2 %copy-start.138 = (f32[2048]{0:T(1024)S(1)}, f32[2048]{0:T(1024)}, u32[]{:S(2)}) copy-start(f32[2048]{0:T(1024)} %get-tuple-element.191) | copy-start | bytes 24580
  949.7 128.7 %copy-start.130 = (bf16[16,2048]{1,0:T(8,128)(2,1)S(1)}, bf16[16,2048]{1,0:T(8,128)(2,1)}, u32[]{:S(2)}) copy-start(bf16[16,2048]{1,0:T(8,128)(2,1)} %get-tuple-element.184) | copy-start | bytes 196612
  949.7 128.7 %copy-start.139 = (f32[2048]{0:T(1024)S(1)}, f32[2048]{0:T(1024)}, u32[]{:S(2)}) copy-start(f32[2048]{0:T(1024)} %get-tuple-element.189) | copy-start | bytes 24580
  (134 other events, 493.3 us)
Sparse Core Ops, SparseCore 0:
  66.3 39.4 all-gather.4
  107.6 36.7 all-gather.6
  237.7 84.2 all-reduce.22
  399.2 85.3 all-reduce.20
  506.8 50.2 reduce-scatter.2
  560.7 51.3 reduce-scatter.4
  658.0 49.6 all-reduce.12
  723.4 52.0 all-reduce.16
  778.9 161.5 all-reduce.18
  947.1 129.6 all-reduce.14
where the time goes:
time: 1100 us; the launch traced here: 1090 us
  waiting for transfers between devices  372 us (34%)
  matrix products  356 us (32%)
  local copies, waits for them, and re-layouts  132 us (12%)
  other arithmetic  127 us (12%)
  blocking collectives  84.2 us (8%)
  between operations  18 us (2%)
    psum x1, waiting for transfers between devices, on_device(): lax.psum((qkv_left, gate_left, output_right_factor, down_right_factor, ou...  126 us
    psum x1, waiting for transfers between devices, on_device(): lax.psum(jnp.dot(hidden, down_weight, preferred_element_type=jnp.float32)...  92.7 us
    psum x1, waiting for transfers between devices, on_device(): lax.psum(contract_cols(gate_up_grad, gate_up_weight).astype(jnp.bfloat16)...  82.5 us
    psum x1, waiting for transfers between devices, on_device(): lax.psum(jnp.dot(attended, out_weight, preferred_element_type=jnp.float32...  70.7 us
    dot_general x8, matrix products, contract_rows(): lax.dot_general(left_factor, right_factor, (((0,), (0,)), ((), ())), pref...  62.3 us
    unnamed x350, local copies, waits for them, and re-layouts  60.3 us
    dot_general x2, matrix products, column_gradient_list(): jnp.einsum('emn,mez->enz', left_factor, merged_matrix_gradient, precision...  42.7 us
    psum x1, blocking collectives, on_device(): lax.psum((qkv_left, gate_left, output_right_factor, down_right_factor, ou...  42.4 us
  transfers between devices with their start and end apart: 10, of which 4 were waited for; matrix products, arithmetic and copies ran while one was open for 40% of the time, Pallas kernels for 0%

commit v1 on v0

--- a/solution.py
+++ b/solution.py
@@ -3,6 +3,8 @@
 import jax
 import jax.numpy as jnp
 from jax import lax
+from jax.experimental import pallas as pl
+from jax.experimental.pallas import tpu as pltpu
 from jax.sharding import PartitionSpec as P
 
 HEAD_DIM = 128
@@ -114,7 +116,7 @@
     return (inner, left_factor_part, right_factor_part)
 
 
-def on_device(
+def general_device(
     inputs,
     lengths,
     prompt_mask,
@@ -498,6 +500,903 @@
     )
 
 
+FAR_SLOTS = 128
+LANES = 128
+VMEM_LIMIT = 56 * 1024 * 1024
+f32 = jnp.float32
+bf16 = jnp.bfloat16
+
+
+def fits_fast(mesh):
+    return mesh.shape["dp"] == 8 and mesh.shape["tensor"] == 4
+
+
+def split_high_low(value):
+    high = value.astype(bf16)
+    return high, (value - high.astype(f32)).astype(bf16)
+
+
+def adapter_product(first_t, second):
+    a_high, a_low = split_high_low(first_t)
+    b_high, b_low = split_high_low(second)
+    left = jnp.concatenate([a_high, a_low, a_high], axis=0)
+    right = jnp.concatenate([b_high, b_high, b_low], axis=0)
+    return contract_rows(left, right)
+
+
+def params(limit=VMEM_LIMIT):
+    return pltpu.CompilerParams(vmem_limit_bytes=limit)
+
+
+def whole_block(shape):
+    zeros = (0,) * len(shape)
+    return pl.BlockSpec(shape, lambda *_: zeros)
+
+
+def merge_in(frozen, first_t, second, row_block):
+    depth, groups, cols = frozen.shape
+    rank = second.shape[1]
+    scale = ADAPTER_NUMER / ADAPTER_RANK
+
+    def kernel(w_ref, a_ref, b_ref, v_ref, sq_ref):
+        @pl.when(pl.program_id(0) == 0)
+        def _():
+            sq_ref[...] = jnp.zeros_like(sq_ref)
+
+        for g in range(groups):
+            v = w_ref[:, g, :].astype(f32) + scale * adapter_product(a_ref[g], b_ref[g])
+            v_ref[:, g * cols : (g + 1) * cols] = v.astype(bf16)
+            sq_ref[:, g * cols : (g + 1) * cols] += jnp.sum(v * v, axis=0, keepdims=True)
+
+    return pl.pallas_call(
+        kernel,
+        grid=(depth // row_block,),
+        in_specs=[
+            pl.BlockSpec((row_block, groups, cols), lambda i: (i, 0, 0)),
+            pl.BlockSpec((groups, rank, row_block), lambda i: (0, 0, i)),
+            whole_block((groups, rank, cols)),
+        ],
+        out_specs=[
+            pl.BlockSpec((row_block, groups * cols), lambda i: (i, 0)),
+            whole_block((1, groups * cols)),
+        ],
+        out_shape=[
+            jax.ShapeDtypeStruct((depth, groups * cols), bf16),
+            jax.ShapeDtypeStruct((1, groups * cols), f32),
+        ],
+        compiler_params=params(),
+        cost_estimate=pl.CostEstimate(
+            flops=2 * depth * groups * cols * 48,
+            bytes_accessed=4 * depth * groups * cols,
+            transcendentals=0,
+        ),
+        name="merge_in",
+    )(frozen, first_t, second)
+
+
+def merge_out(frozen, first_t, second, row_block):
+    depth, cols = frozen.shape
+    rank = second.shape[0]
+    scale = ADAPTER_NUMER / ADAPTER_RANK
+
+    def kernel(w_ref, a_ref, b_ref, v_ref, sq_ref):
+        @pl.when(pl.program_id(0) == 0)
+        def _():
+            sq_ref[...] = jnp.zeros_like(sq_ref)
+
+        v = w_ref[...].astype(f32) + scale * adapter_product(a_ref[...], b_ref[...])
+        v_ref[...] = v.astype(bf16)
+        sq_ref[...] += jnp.sum(v * v, axis=0, keepdims=True)
+
+    return pl.pallas_call(
+        kernel,
+        grid=(depth // row_block,),
+        in_specs=[
+            pl.BlockSpec((row_block, cols), lambda i: (i, 0)),
+            pl.BlockSpec((rank, row_block), lambda i: (0, i)),
+            whole_block((rank, cols)),
+        ],
+        out_specs=[pl.BlockSpec((row_block, cols), lambda i: (i, 0)), whole_block((1, cols))],
+        out_shape=[
+            jax.ShapeDtypeStruct((depth, cols), bf16),
+            jax.ShapeDtypeStruct((1, cols), f32),
+        ],
+        compiler_params=params(),
+        cost_estimate=pl.CostEstimate(
+            flops=2 * depth * cols * 48, bytes_accessed=4 * depth * cols, transcendentals=0
+        ),
+        name="merge_out",
+    )(frozen, first_t, second)
+
+
+def rotate(values, cosine, sine_signed):
+    return values * cosine + pltpu.roll(values, HEAD_DIM // 2, 1) * sine_signed
+
+
+def rotate_back(values, cosine, sine_signed):
+    return values * cosine - pltpu.roll(values, HEAD_DIM // 2, 1) * sine_signed
+
+
+def project_in(tokens, gain, merged, ratio, cosine, sine_signed):
+    count, width = tokens.shape
+    cols = merged.shape[1] // 3
+    heads = cols // HEAD_DIM
+
+    def kernel(x_ref, g_ref, w_ref, s_ref, c_ref, n_ref, a_ref, y_ref):
+        part = pl.program_id(0)
+
+        @pl.when(part == 0)
+        def _():
+            x = x_ref[...].astype(f32)
+            a_ref[...] = (x * rms_scale(x) * g_ref[...]).astype(bf16)
+
+        y = jnp.dot(a_ref[...], w_ref[...], preferred_element_type=f32) * s_ref[...]
+
+        @pl.when(part < 2)
+        def _():
+            for h in range(heads):
+                at = slice(h * HEAD_DIM, (h + 1) * HEAD_DIM)
+                y_ref[:, at] = rotate(y[:, at], c_ref[...], n_ref[...]).astype(bf16)
+
+        @pl.when(part == 2)
+        def _():
+            y_ref[...] = y.astype(bf16)
+
+    return pl.pallas_call(
+        kernel,
+        grid=(3,),
+        in_specs=[
+            whole_block((count, width)),
+            whole_block((1, width)),
+            pl.BlockSpec((width, cols), lambda i: (0, i)),
+            pl.BlockSpec((1, cols), lambda i: (0, i)),
+            whole_block((count, HEAD_DIM)),
+            whole_block((count, HEAD_DIM)),
+        ],
+        out_specs=[whole_block((count, width)), pl.BlockSpec((count, cols), lambda i: (0, i))],
+        out_shape=[
+            jax.ShapeDtypeStruct((count, width), bf16),
+            jax.ShapeDtypeStruct((count, 3 * cols), bf16),
+        ],
+        compiler_params=params(),
+        cost_estimate=pl.CostEstimate(
+            flops=2 * count * width * 3 * cols,
+            bytes_accessed=2 * (2 * count * width + 3 * cols * (width + count)),
+            transcendentals=0,
+        ),
+        name="project_in",
+    )(tokens, gain, merged, ratio, cosine, sine_signed)
+
+
+def head_shares(q, k, far_k, far_ok):
+    scale = 1.0 / math.sqrt(HEAD_DIM)
+    own = contract_cols(q, k) * scale
+    far = contract_cols(q, far_k) * scale
+    rows_at = lax.broadcasted_iota(jnp.int32, own.shape, 0)
+    slots_at = lax.broadcasted_iota(jnp.int32, own.shape, 1)
+    own = jnp.where(slots_at <= rows_at, own, masked_score)
+    far = jnp.where(far_ok > 0, far, masked_score)
+    scores = jnp.concatenate([own, far], axis=1)
+    top = jnp.max(scores, axis=-1, keepdims=True)
+    exponent = jnp.exp(scores - top)
+    return exponent / jnp.sum(exponent, axis=-1, keepdims=True)
+
+
+def store_part(value, refs, inner):
+    if len(refs) == 1:
+        refs[0][...] = value
+        return
+    half = value.shape[0] // 2
+
+    @pl.when(inner == 1)
+    def _():
+        refs[0][...] = value[half:]
+        refs[1][...] = value[:half]
+
+    @pl.when(inner != 1)
+    def _():
+        refs[0][...] = value[:half]
+        refs[1][...] = value[half:]
+
+
+def load_total(refs, inner):
+    if len(refs) == 1:
+        return refs[0][...].astype(f32)
+    mine, other = refs[0][...], refs[1][...]
+    flip = inner == 1
+    first = jnp.where(flip, other, mine)
+    last = jnp.where(flip, mine, other)
+    return jnp.concatenate([first, last], axis=0).astype(f32)
+
+
+def part_shapes(slots, width, pieces):
+    return [jax.ShapeDtypeStruct((slots // pieces, width), bf16)] * pieces
+
+
+def attend(inner, projected, far_pack, out_merged, pieces):
+    slots = projected.shape[0]
+    cols = projected.shape[1] // 3
+    heads = cols // HEAD_DIM
+    width = out_merged.shape[1]
+
+    def kernel(i_ref, y_ref, f_ref, w_ref, o_ref, *z_refs):
+        far_ok = f_ref[FAR_SLOTS : FAR_SLOTS + 1, :FAR_SLOTS].astype(f32)
+        for h in range(heads):
+            at = slice(h * HEAD_DIM, (h + 1) * HEAD_DIM)
+            far_k = f_ref[:FAR_SLOTS, h * HEAD_DIM : (h + 1) * HEAD_DIM]
+            far_v = f_ref[:FAR_SLOTS, cols + h * HEAD_DIM : cols + (h + 1) * HEAD_DIM]
+            k = y_ref[:, cols + h * HEAD_DIM : cols + (h + 1) * HEAD_DIM]
+            v = y_ref[:, 2 * cols + h * HEAD_DIM : 2 * cols + (h + 1) * HEAD_DIM]
+            shares = head_shares(y_ref[:, at], k, far_k, far_ok).astype(bf16)
+            values = jnp.concatenate([v, far_v], axis=0)
+            o_ref[:, at] = jnp.dot(shares, values, preferred_element_type=f32).astype(bf16)
+        part = jnp.dot(o_ref[...], w_ref[...], preferred_element_type=f32).astype(bf16)
+        store_part(part, z_refs, i_ref[0])
+
+    return pl.pallas_call(
+        kernel,
+        in_specs=[pl.BlockSpec(memory_space=pltpu.SMEM)]
+        + [pl.BlockSpec(memory_space=pltpu.VMEM)] * 3,
+        out_shape=[jax.ShapeDtypeStruct((slots, cols), bf16)]
+        + part_shapes(slots, width, pieces),
+        compiler_params=params(),
+        cost_estimate=pl.CostEstimate(
+            flops=2 * slots * cols * (width + 2 * (slots + FAR_SLOTS)),
+            bytes_accessed=2 * (cols * width + slots * (4 * cols + width)),
+            transcendentals=heads * slots * (slots + FAR_SLOTS),
+        ),
+        name="attend",
+    )(inner, projected, far_pack, out_merged)
+
+
+def feed_forward(
+    scalars, branch_sum, tokens, upstream, out_ratio, down_ratio, gain, merged, ratio, down_merged
+):
+    slots, width = tokens.shape
+    units = down_merged.shape[0]
+    blocks = units // LANES
+    pieces = len(branch_sum)
+
+    def kernel(*refs):
+        n_ref, *refs = refs
+        s_refs, refs = refs[:pieces], refs[pieces:]
+        x_ref, u_ref, or_ref, dr_ref, g_ref, wg_ref, wu_ref, rg_ref, ru_ref, wd_ref = refs[:10]
+        h_ref, b_ref, d2_ref, hid_ref, dg_ref, du_ref, cg_ref, cu_ref, cd_ref, y_ref = refs[10:20]
+        db_refs, (dba_ref, ya_ref) = refs[20:-2], refs[-2:]
+        at = pl.program_id(0)
+
+        def live_rows():
+            return lax.broadcasted_iota(jnp.int32, (slots, 1), 0) < n_ref[0]
+
+        @pl.when(at == 0)
+        def _():
+            live = live_rows()
+            branch = load_total(s_refs, n_ref[1]) * or_ref[...]
+            h = x_ref[...].astype(f32) + jnp.where(live, branch, 0.0)
+            h_ref[...] = h
+            b_ref[...] = (h * rms_scale(h) * g_ref[...]).astype(bf16)
+            d2_ref[...] = jnp.where(live, u_ref[...].astype(f32) * dr_ref[...], 0.0).astype(bf16)
+            dba_ref[...] = jnp.zeros_like(dba_ref)
+            ya_ref[...] = jnp.zeros_like(ya_ref)
+
+        weight = jnp.concatenate([wg_ref[...], wu_ref[...]], axis=1)
+        raw = jnp.dot(b_ref[...], weight, preferred_element_type=f32)
+        gate = raw[:, :LANES] * rg_ref[...]
+        up = raw[:, LANES:] * ru_ref[...]
+        sigmoid = jax.nn.sigmoid(gate)
+        activated = gate * sigmoid
+        hidden = (activated * up).astype(bf16)
+        hid_ref[...] = hidden
+        dhidden = contract_cols(d2_ref[...], wd_ref[...])
+        dgate = dhidden * up * sigmoid * (1.0 + gate * (1.0 - sigmoid))
+        dup = dhidden * activated
+        cg_ref[...] = jnp.sum(dgate * raw[:, :LANES], axis=0, keepdims=True)
+        cu_ref[...] = jnp.sum(dup * raw[:, LANES:], axis=0, keepdims=True)
+        dgate = (dgate * rg_ref[...]).astype(bf16)
+        dup = (dup * ru_ref[...]).astype(bf16)
+        dg_ref[...] = dgate
+        du_ref[...] = dup
+        dba_ref[...] += contract_cols(jnp.concatenate([dgate, dup], axis=1), weight)
+        ya_ref[...] += jnp.dot(hidden, wd_ref[...], preferred_element_type=f32)
+
+        @pl.when(at == blocks - 1)
+        def _():
+            store_part(dba_ref[...].astype(bf16), db_refs, n_ref[1])
+            y_ref[...] = ya_ref[...].astype(bf16)
+            d2 = jnp.where(live_rows(), u_ref[...].astype(f32), 0.0)
+            cd_ref[...] = jnp.sum(d2 * ya_ref[...], axis=0, keepdims=True)
+
+    row = whole_block((1, width))
+    full = whole_block((slots, width))
+    part = whole_block((slots // pieces, width))
+    unit_cols = pl.BlockSpec((slots, LANES), lambda i: (0, i))
+    unit_row = pl.BlockSpec((1, LANES), lambda i: (0, i))
+    return pl.pallas_call(
+        kernel,
+        grid=(blocks,),
+        in_specs=[pl.BlockSpec(memory_space=pltpu.SMEM)]
+        + [part] * pieces
+        + [
+            full,
+            full,
+            row,
+            row,
+            row,
+            pl.BlockSpec((width, LANES), lambda i: (0, i)),
+            pl.BlockSpec((width, LANES), lambda i: (0, blocks + i)),
+            unit_row,
+            pl.BlockSpec((1, LANES), lambda i: (0, blocks + i)),
+            pl.BlockSpec((LANES, width), lambda i: (i, 0)),
+        ],
+        out_specs=[full] * 3 + [unit_cols] * 3 + [unit_row] * 2 + [row, full] + [part] * pieces,
+        out_shape=[
+            jax.ShapeDtypeStruct((slots, width), f32),
+            jax.ShapeDtypeStruct((slots, width), bf16),
+            jax.ShapeDtypeStruct((slots, width), bf16),
+            jax.ShapeDtypeStruct((slots, units), bf16),
+            jax.ShapeDtypeStruct((slots, units), bf16),
+            jax.ShapeDtypeStruct((slots, units), bf16),
+            jax.ShapeDtypeStruct((1, units), f32),
+            jax.ShapeDtypeStruct((1, units), f32),
+            jax.ShapeDtypeStruct((1, width), f32),
+            jax.ShapeDtypeStruct((slots, width), bf16),
+        ]
+        + part_shapes(slots, width, pieces),
+        scratch_shapes=[
+            pltpu.VMEM((slots, width), f32),
+            pltpu.VMEM((slots, width), f32),
+        ],
+        compiler_params=params(),
+        cost_estimate=pl.CostEstimate(
+            flops=2 * slots * width * units * 6,
+            bytes_accessed=2 * 3 * width * units + 16 * slots * width,
+            transcendentals=slots * units,
+        ),
+        name="feed_forward",
+    )(
+        scalars,
+        *branch_sum,
+        tokens,
+        upstream,
+        out_ratio,
+        down_ratio,
+        gain,
+        merged,
+        merged,
+        ratio,
+        ratio,
+        down_merged,
+    )
+
+
+def attend_back(
+    scalars,
+    db_sum,
+    middle,
+    upstream,
+    branch_sum,
+    gain,
+    out_ratio,
+    out_merged,
+    projected,
+    far_pack,
+    cosine,
+    sine_signed,
+):
+    slots, width = middle.shape
+    cols = projected.shape[1] // 3
+    heads = cols // HEAD_DIM
+    scale = 1.0 / math.sqrt(HEAD_DIM)
+    pieces = len(db_sum)
+
+    def kernel(*refs):
+        n_ref, *refs = refs
+        e_refs, s_refs, refs = refs[:pieces], refs[pieces : 2 * pieces], refs[2 * pieces :]
+        h_ref, u_ref, g_ref, or_ref, w_ref, y_ref, f_ref, c_ref, sn_ref = refs[:9]
+        dh_ref, d1_ref, co_ref, dy_ref, far_ref, do_ref = refs[9:]
+        live = lax.broadcasted_iota(jnp.int32, (slots, 1), 0) < n_ref[0]
+        h = h_ref[...]
+        back = rms_back(h, rms_scale(h), g_ref[...], load_total(e_refs, n_ref[1]))
+        dh = u_ref[...].astype(f32) + back
+        dh_ref[...] = dh
+        d1 = jnp.where(live, dh, 0.0)
+        co_ref[...] = jnp.sum(d1 * load_total(s_refs, n_ref[1]), axis=0, keepdims=True)
+        d1_ref[...] = (d1 * or_ref[...]).astype(bf16)
+        do_ref[...] = contract_cols(d1_ref[...], w_ref[...]).astype(bf16)
+        far_ok = f_ref[FAR_SLOTS : FAR_SLOTS + 1, :FAR_SLOTS].astype(f32)
+        for i in range(heads):
+            at = slice(i * HEAD_DIM, (i + 1) * HEAD_DIM)
+            k_at = slice(cols + i * HEAD_DIM, cols + (i + 1) * HEAD_DIM)
+            v_at = slice(2 * cols + i * HEAD_DIM, 2 * cols + (i + 1) * HEAD_DIM)
+            q = y_ref[:, at]
+            far_k = f_ref[:FAR_SLOTS, at]
+            shares = head_shares(q, y_ref[:, k_at], far_k, far_ok)
+            keys = jnp.concatenate([y_ref[:, k_at], far_k], axis=0)
+            values = jnp.concatenate([y_ref[:, v_at], f_ref[:FAR_SLOTS, k_at]], axis=0)
+            do = do_ref[:, at]
+            share_grad = contract_cols(do, values)
+            inner = jnp.sum(shares * share_grad, axis=-1, keepdims=True)
+            score_grad = (shares * (share_grad - inner)).astype(bf16)
+            dq = jnp.dot(score_grad, keys, preferred_element_type=f32) * scale
+            dk = contract_rows(score_grad, q) * scale
+            dv = contract_rows(shares.astype(bf16), do)
+            dy_ref[:, at] = rotate_back(dq, c_ref[...], sn_ref[...])
+            dy_ref[:, k_at] = dk[:slots]
+            dy_ref[:, v_at] = dv[:slots]
+            far_ref[:, at] = dk[slots:].astype(bf16)
+            far_ref[:, k_at] = dv[slots:].astype(bf16)
+
+    operands = (
+        scalars,
+        *db_sum,
+        *branch_sum,
+        middle,
+        upstream,
+        gain,
+        out_ratio,
+        out_merged,
+        projected,
+        far_pack,
+        cosine,
+        sine_signed,
+    )
+    return pl.pallas_call(
+        kernel,
+        in_specs=[pl.BlockSpec(memory_space=pltpu.SMEM)]
+        + [pl.BlockSpec(memory_space=pltpu.VMEM)] * (len(operands) - 1),
+        out_shape=[
+            jax.ShapeDtypeStruct((slots, width), f32),
+            jax.ShapeDtypeStruct((slots, width), bf16),
+            jax.ShapeDtypeStruct((1, width), f32),
+            jax.ShapeDtypeStruct((slots, 3 * cols), f32),
+            jax.ShapeDtypeStruct((FAR_SLOTS, 2 * cols), bf16),
+        ],
+        scratch_shapes=[pltpu.VMEM((slots, cols), bf16)],
+        compiler_params=params(),
+        cost_estimate=pl.CostEstimate(
+            flops=2 * slots * cols * (width + 5 * (slots + FAR_SLOTS)),
+            bytes_accessed=2 * (cols * width + slots * (8 * width + 9 * cols)),
+            transcendentals=heads * slots * (slots + FAR_SLOTS),
+        ),
+        name="attend_back",
+    )(*operands)
+
+
+def project_back(inner, dy, returned, projected, cosine, sine_signed, ratio, merged, pieces):
+    slots, total = dy.shape
+    cols = total // 3
+    heads = cols // HEAD_DIM
+    width = merged.shape[0]
+    blocks = 4
+    step = width // blocks
+
+    def kernel(i_ref, d_ref, r_ref, y_ref, c_ref, sn_ref, s_ref, w_ref, o_ref, cs_ref, *da_refs):
+        @pl.when(pl.program_id(0) == 0)
+        def _():
+            for i in range(3 * heads):
+                at = slice(i * HEAD_DIM, (i + 1) * HEAD_DIM)
+                d = d_ref[:, at]
+                raw = y_ref[:, at].astype(f32)
+                if i >= heads:
+                    back = slice((i - heads) * HEAD_DIM, (i - heads + 1) * HEAD_DIM)
+                    low = d[:FAR_SLOTS] + r_ref[:FAR_SLOTS, back].astype(f32)
+                    d = jnp.concatenate([low, d[FAR_SLOTS:]], axis=0)
+                if heads <= i < 2 * heads:
+                    d = rotate_back(d, c_ref[...], sn_ref[...])
+                if i < 2 * heads:
+                    raw = rotate_back(raw, c_ref[...], sn_ref[...])
+                cs_ref[:, at] = jnp.sum(d * raw, axis=0, keepdims=True)
+                o_ref[:, at] = (d * s_ref[:, at]).astype(bf16)
+
+        store_part(contract_cols(o_ref[...], w_ref[...]).astype(bf16), da_refs, i_ref[0])
+
+    return pl.pallas_call(
+        kernel,
+        grid=(blocks,),
+        in_specs=[
+            pl.BlockSpec(memory_space=pltpu.SMEM),
+            whole_block((slots, total)),
+            whole_block(returned.shape),
+            whole_block((slots, total)),
+            whole_block((slots, HEAD_DIM)),
+            whole_block((slots, HEAD_DIM)),
+            whole_block((1, total)),
+            pl.BlockSpec((step, total), lambda i: (i, 0)),
+        ],
+        out_specs=[
+            whole_block((slots, total)),
+            whole_block((1, total)),
+        ]
+        + [pl.BlockSpec((slots // pieces, step), lambda i: (0, i))] * pieces,
+        out_shape=[
+            jax.ShapeDtypeStruct((slots, total), bf16),
+            jax.ShapeDtypeStruct((1, total), f32),
+        ]
+        + part_shapes(slots, width, pieces),
+        compiler_params=params(),
+        cost_estimate=pl.CostEstimate(
+            flops=2 * slots * total * width,
+            bytes_accessed=2 * (total * width + slots * (width + 5 * total)),
+            transcendentals=0,
+        ),
+        name="project_back",
+    )(inner, dy, returned, projected, cosine, sine_signed, ratio, merged)
+
+
+LINE_PAIRS = [(0, 1), (1, 0), (2, 3), (3, 2)]
+LINE_ACROSS = [(0, 3), (3, 0), (1, 2), (2, 1)]
+
+
+def tensor_sum(parts):
+    if len(parts) == 1:
+        return [lax.psum(parts[0], "tensor")]
+    keep, send = parts
+    pair = keep + lax.ppermute(send, "tensor", LINE_PAIRS)
+    total = pair + lax.ppermute(pair, "tensor", LINE_ACROSS)
+    return [total, lax.ppermute(total, "tensor", LINE_PAIRS)]
+
+
+def line_total(value):
+    value = value + lax.ppermute(value, "tensor", LINE_PAIRS)
+    return value + lax.ppermute(value, "tensor", LINE_ACROSS)
+
+
+def dp_total(value, line_rows):
+    me = lax.axis_index("dp")
+    hops = (1, 2, 4)
+    for hop in hops:
+        half = value.shape[1] // 2
+        low, high = value[:, :half], value[:, half:]
+        upper = (me & hop) != 0
+        keep = jnp.where(upper, high, low)
+        send = jnp.where(upper, low, high)
+        value = keep + lax.ppermute(send, "dp", [(i, i ^ hop) for i in range(8)])
+    value = jnp.concatenate([line_total(value[:line_rows]), value[line_rows:]], axis=0)
+    for hop in reversed(hops):
+        upper = (me & hop) != 0
+        other = lax.ppermute(value, "dp", [(i, i ^ hop) for i in range(8)])
+        value = jnp.concatenate(
+            [jnp.where(upper, other, value), jnp.where(upper, value, other)], axis=1
+        )
+    return value.astype(f32)
+
+
+def pair_exchange(pack, distance, sibling_distance):
+    held = [pack] + [
+        lax.ppermute(pack, "dp", [(i, i ^ hop) for i in range(8)]) for hop in (2, 4, 6)
+    ]
+
+    def pick(index):
+        return lax.select_n(index // 2, *held)
+
+    asked = pick(sibling_distance & 6)
+    across = lax.ppermute(asked, "dp", [(i, i ^ 1) for i in range(8)])
+    return jnp.where(distance % 2 == 1, across, pick(distance & 6))
+
+
+def block_rows_of(second, groups):
+    rank, cols = second.shape[1:]
+    parts = []
+    for g in range(groups):
+        parts.append(jnp.pad(second[g], ((g * rank, (groups - 1 - g) * rank), (0, 0))))
+    return jnp.concatenate(parts, axis=1)
+
+
+def low_dot(left, right, dims):
+    return lax.dot_general(
+        left.astype(bf16), right.astype(bf16), (dims, ((), ())), preferred_element_type=f32
+    )
+
+
+def adapter_in(inputs_seen, grads_scaled, inner, square, magnitude, merged, first_t, second):
+    groups, rank, cols = second.shape
+    scale = ADAPTER_NUMER / ADAPTER_RANK
+    norm = jnp.sqrt(square)
+    share = inner * magnitude / (square * norm)
+    wide = block_rows_of(second, groups)
+    tall = first_t.reshape(groups * rank, -1)
+    seen = low_dot(inputs_seen, tall, ((1,), (1,)))
+    sent = low_dot(grads_scaled, wide, ((1,), (1,)))
+    left = low_dot(sent, inputs_seen, ((0,), (0,))) - low_dot(wide * share, merged, ((1,), (1,)))
+    right = low_dot(seen, grads_scaled, ((0,), (0,))) - low_dot(tall, merged, ((1,), (0,))) * share
+    right = jnp.stack(
+        [right[g * rank : (g + 1) * rank, g * cols : (g + 1) * cols] for g in range(groups)]
+    )
+    return (
+        scale * left.reshape(groups, rank, -1),
+        scale * right,
+        (inner / norm).reshape(groups, cols),
+    )
+
+
+def adapter_out(inputs_seen, grads_scaled, inner, square, magnitude, merged, first_t, second):
+    scale = ADAPTER_NUMER / ADAPTER_RANK
+    norm = jnp.sqrt(square)
+    share = inner * magnitude / (square * norm)
+    seen = low_dot(inputs_seen, first_t, ((1,), (1,)))
+    sent = low_dot(grads_scaled, second, ((1,), (1,)))
+    left = low_dot(sent, inputs_seen, ((0,), (0,))) - low_dot(second * share, merged, ((1,), (1,)))
+    right = (
+        low_dot(seen, grads_scaled, ((0,), (0,))) - low_dot(first_t, merged, ((1,), (0,))) * share
+    )
+    return scale * left, scale * right, inner / norm
+
+
+def fast_device(
+    inputs,
+    lengths,
+    prompt_mask,
+    partner,
+    positions,
+    attn_gain,
+    mlp_gain,
+    attention_input_frozen,
+    attention_input_first,
+    attention_input_second,
+    attention_input_magnitude,
+    attention_output_frozen,
+    attention_output_first,
+    attention_output_second,
+    attention_output_magnitude,
+    feedforward_input_frozen,
+    feedforward_input_first,
+    feedforward_input_second,
+    feedforward_input_magnitude,
+    feedforward_output_frozen,
+    feedforward_output_first,
+    feedforward_output_second,
+    feedforward_output_magnitude,
+    grad_out,
+):
+    micros, _, slots, width = inputs.shape
+    cols = attention_input_frozen.shape[2]
+    attn_row = attn_gain.astype(f32)[None]
+    mlp_row = mlp_gain.astype(f32)[None]
+    qkv_first_t = jnp.swapaxes(attention_input_first, 1, 2)
+    gate_first_t = jnp.swapaxes(feedforward_input_first, 1, 2)
+    out_first_t = attention_output_first.T
+    down_first_t = feedforward_output_first.T
+    qkv_magnitude = attention_input_magnitude.reshape(1, -1)
+    gate_magnitude = feedforward_input_magnitude.reshape(1, -1)
+    out_magnitude = attention_output_magnitude[None]
+    down_magnitude = feedforward_output_magnitude[None]
+
+    me = lax.axis_index("dp")
+    distance = partner[:, 0] ^ me
+    sibling_distance = lax.ppermute(distance, "dp", [(i, i ^ 1) for i in range(8)])
+
+    qkv_merged, qkv_square = merge_in(
+        attention_input_frozen, qkv_first_t, attention_input_second, 256
+    )
+    qkv_ratio = qkv_magnitude * lax.rsqrt(qkv_square)
+    indices = jnp.arange(HEAD_DIM // 2, dtype=f32)
+    inverse = rope_base ** (-2.0 * indices / HEAD_DIM)
+    angles = positions.reshape(micros * slots).astype(f32)[:, None] * inverse[None, :]
+    cosine, sine = jnp.cos(angles), jnp.sin(angles)
+    cosine = jnp.concatenate([cosine, cosine], axis=1)
+    sine_signed = jnp.concatenate([-sine, sine], axis=1)
+    tokens = inputs.reshape(micros * slots, width)
+    upstream = grad_out.reshape(micros * slots, width)
+    normed, projected = project_in(
+        tokens, attn_row, qkv_merged, qkv_ratio, cosine, sine_signed
+    )
+
+    def rows(array, micro_at):
+        return array[micro_at * slots : (micro_at + 1) * slots]
+
+    far_packs = []
+    for m in range(micros):
+        flags = prompt_mask[m, :, :FAR_SLOTS].astype(bf16)
+        flags = jnp.pad(flags, ((0, 15), (0, 2 * cols - FAR_SLOTS)))
+        pack = jnp.concatenate([rows(projected, m)[:FAR_SLOTS, cols:], flags], axis=0)
+        far_packs.append(pair_exchange(pack, distance[m], sibling_distance[m]))
+
+    out_merged, out_square = merge_out(
+        attention_output_frozen, out_first_t, attention_output_second, 256
+    )
+    down_merged, down_square = merge_out(
+        feedforward_output_frozen, down_first_t, feedforward_output_second, 128
+    )
+    pieces = (2, 1)
+    line_at = lax.axis_index("tensor")
+    inner = ((line_at == 1) | (line_at == 2)).astype(jnp.int32)[None]
+    scalars = [jnp.concatenate([lengths[m], inner]) for m in range(micros)]
+    squares = line_total(jnp.concatenate([out_square, down_square], axis=0))
+    out_square, down_square = squares[:1], squares[1:]
+    out_ratio = out_magnitude * lax.rsqrt(out_square)
+    down_ratio = down_magnitude * lax.rsqrt(down_square)
+
+    attended, branch_sums = [], []
+    for m in range(micros):
+        seen, *part = attend(inner, rows(projected, m), far_packs[m], out_merged, pieces[m])
+        attended.append(seen)
+        branch_sums.append(tensor_sum(part))
+    gate_second, _ = lax.optimization_barrier((feedforward_input_second, attended[0]))
+    gate_merged, gate_square = merge_in(feedforward_input_frozen, gate_first_t, gate_second, 128)
+    gate_ratio = gate_magnitude * lax.rsqrt(gate_square)
+
+    middles, normed_mlp, hiddens, gate_grads, gate_inner = [], [], [], [], 0.0
+    db_sums, down_parts, down_grads, down_inner = [], [], [], 0.0
+    for m in range(micros):
+        middle, b, d2, hidden, dgate, dup, c_gate, c_up, c_down, y, *db = feed_forward(
+            scalars[m],
+            branch_sums[m],
+            rows(tokens, m),
+            rows(upstream, m),
+            out_ratio,
+            down_ratio,
+            mlp_row,
+            gate_merged,
+            gate_ratio,
+            down_merged,
+        )
+        middles.append(middle)
+        normed_mlp.append(b)
+        hiddens.append(hidden)
+        gate_grads.append(jnp.concatenate([dgate, dup], axis=1))
+        gate_inner = gate_inner + jnp.concatenate([c_gate, c_up], axis=1)
+        down_inner = down_inner + c_down
+        down_grads.append(d2)
+        db_sums.append(tensor_sum(db))
+        down_parts.append(y)
+    down_inner = line_total(down_inner)
+
+    middle_grads, out_grads, out_inner, qkv_grads, qkv_inner, da_sums = [], [], 0.0, [], 0.0, []
+    for m in range(micros):
+        dh, d1, c_out, dy, far_grad = attend_back(
+            scalars[m],
+            db_sums[m],
+            middles[m],
+            rows(upstream, m),
+            branch_sums[m],
+            mlp_row,
+            out_ratio,
+            out_merged,
+            rows(projected, m),
+            far_packs[m],
+            rows(cosine, m),
+            rows(sine_signed, m),
+        )
+        middle_grads.append(dh)
+        out_grads.append(d1)
+        out_inner = out_inner + c_out
+        returned = pair_exchange(far_grad, distance[m], sibling_distance[m])
+        dqkv, c_qkv, *da = project_back(
+            inner,
+            dy,
+            returned,
+            rows(projected, m),
+            rows(cosine, m),
+            rows(sine_signed, m),
+            qkv_ratio,
+            qkv_merged,
+            2,
+        )
+        qkv_grads.append(dqkv)
+        qkv_inner = qkv_inner + c_qkv
+        da_sums.append(tensor_sum(da))
+    down_sums = [tensor_sum([y])[0] for y in down_parts]
+
+    def assemble(total):
+        if len(total) == 1:
+            return total[0].astype(f32)
+        first = jnp.where(inner[0] == 1, total[1], total[0])
+        last = jnp.where(inner[0] == 1, total[0], total[1])
+        return jnp.concatenate([first, last], axis=0).astype(f32)
+
+    results, input_grads = [], []
+    for m in range(micros):
+        live = (jnp.arange(slots) < lengths[m, 0])[:, None]
+        branch = down_sums[m].astype(f32) * down_ratio
+        results.append((middles[m] + jnp.where(live, branch, 0.0)).astype(bf16))
+        x = rows(tokens, m).astype(f32)
+        back = rms_back(x, rms_scale(x), attn_row, assemble(da_sums[m]))
+        input_grads.append((middle_grads[m] + back).astype(bf16))
+
+    units = feedforward_input_frozen.shape[2]
+    gate_left, gate_right, gate_mag = adapter_in(
+        jnp.concatenate(normed_mlp, axis=0),
+        jnp.concatenate(gate_grads, axis=0),
+        gate_inner,
+        gate_square,
+        gate_magnitude,
+        gate_merged,
+        gate_first_t,
+        feedforward_input_second,
+    )
+    down_left, down_right, down_mag = adapter_out(
+        jnp.concatenate(hiddens, axis=0),
+        jnp.concatenate(down_grads, axis=0),
+        down_inner,
+        down_square,
+        down_magnitude,
+        down_merged,
+        down_first_t,
+        feedforward_output_second,
+    )
+    rank = down_left.shape[0]
+
+    def stack_rows(pieces, height):
+        wide = [jnp.pad(p.astype(bf16), ((0, 0), (0, width - p.shape[1]))) for p in pieces]
+        total = jnp.concatenate(wide, axis=0)
+        return jnp.pad(total, ((0, height - total.shape[0]), (0, 0)))
+
+    early = stack_rows(
+        [
+            gate_left.reshape(2 * rank, width),
+            down_right,
+            gate_right.reshape(2 * rank, units),
+            down_left,
+            gate_mag,
+            down_mag,
+        ],
+        7 * rank,
+    )
+    early = dp_total(early, 3 * rank)
+    gate_left = early[: 2 * rank].reshape(2, rank, width)
+    down_right = early[2 * rank : 3 * rank]
+    gate_right = early[3 * rank : 5 * rank, :units].reshape(2, rank, units)
+    down_left = early[5 * rank : 6 * rank, :units]
+    gate_mag = early[6 * rank : 6 * rank + 2, :units]
+    down_mag = early[6 * rank + 2]
+
+    out_left, out_right, out_mag = adapter_out(
+        jnp.concatenate(attended, axis=0),
+        jnp.concatenate(out_grads, axis=0),
+        out_inner,
+        out_square,
+        out_magnitude,
+        out_merged,
+        out_first_t,
+        attention_output_second,
+    )
+    qkv_left, qkv_right, qkv_mag = adapter_in(
+        normed,
+        jnp.concatenate(qkv_grads, axis=0),
+        qkv_inner / qkv_ratio,
+        qkv_square,
+        qkv_magnitude,
+        qkv_merged,
+        qkv_first_t,
+        attention_input_second,
+    )
+    late = stack_rows(
+        [
+            qkv_left.reshape(3 * rank, width),
+            out_right,
+            jnp.concatenate([qkv_right[0], qkv_right[1], qkv_right[2], out_left], axis=1),
+            qkv_mag.reshape(1, 3 * cols),
+            out_mag,
+        ],
+        6 * rank,
+    )
+    late = dp_total(late, 4 * rank)
+    qkv_left = late[: 3 * rank].reshape(3, rank, width)
+    out_right = late[3 * rank : 4 * rank]
+    rights = late[4 * rank : 5 * rank]
+    qkv_right = jnp.stack([rights[:, g * cols : (g + 1) * cols] for g in range(3)])
+    out_left = rights[:, 3 * cols :]
+    qkv_mag = late[5 * rank, : 3 * cols].reshape(3, cols)
+    out_mag = late[5 * rank + 1]
+
+    return (
+        jnp.stack(results)[:, None],
+        jnp.stack(input_grads)[:, None],
+        jnp.swapaxes(qkv_left, 1, 2),
+        qkv_right,
+        qkv_mag,
+        out_left.T,
+        out_right,
+        out_mag,
+        jnp.swapaxes(gate_left, 1, 2),
+        gate_right,
+        gate_mag,
+        down_left.T,
+        down_right,
+        down_mag,
+    )
+
+
 def solution(mesh):
     in_specs = (
         P(None, "dp", None, None),
@@ -541,6 +1440,7 @@
         P(),
         P(),
     )
+    device_step = fast_device if fits_fast(mesh) else general_device
     return jax.shard_map(
-        on_device, mesh=mesh, in_specs=in_specs, out_specs=out_specs, check_vma=False
-    )
+        device_step, mesh=mesh, in_specs=in_specs, out_specs=out_specs, check_vma=False
+    )

time: 1100 us -> 609 us (0.55)
  matrix products: 356 us -> 54.3 us
  waiting for transfers between devices: 372 us -> 149 us
  Pallas kernels: 0 us -> 149 us
  starting transfers between devices: 1.44 us -> 121 us
  local copies, waits for them, and re-layouts: 132 us -> 43.4 us
  blocking collectives: 84.2 us -> 0 us
  other arithmetic: 127 us -> 61 us
    psum x6 -> x2, waiting for transfers between devices: 372 us -> 0.01 us  [tensor_sum(): return [lax.psum(parts[0], 'tensor')]]
    dot_general x50 -> x16, matrix products: 349 us -> 54.3 us  [low_dot(): lax.dot_general(left.astype(bf16), right.astype(bf16), (dims, ((), ())),...]
    ppermute x0 -> x49, waiting for transfers between devices: none -> 149 us  [the longest x4 48.8 us: tensor_sum(): total = pair + lax.ppermute(pair, 'tensor', LINE_ACROSS)]
    pallas_call x0 -> x13, Pallas kernels: none -> 149 us  [the longest x2 48.5 us: feed_forward(): pl.pallas_call(kernel, grid=(blocks,), in_specs=[pl.BlockSpec(memory_spac...]
    ppermute x0 -> x49, starting transfers between devices: none -> 121 us  [the longest x4 68.8 us: tensor_sum(): return [total, lax.ppermute(total, 'tensor', LINE_PAIRS)]]
    psum x3 -> x0, blocking collectives: 65.1 us -> none  [the longest x1 42.4 us: on_device(): lax.psum((qkv_left, gate_left, output_right_factor, down_right_factor, ou...]
    convert_element_type x32 -> x10, other arithmetic: 62.2 us -> 5.67 us  [the longest x4 3.52 us: stack_rows(): p.astype(bf16)]
    unnamed x350 -> x187, local copies, waits for them, and re-layouts: 60.3 us -> 20 us
  transfers between devices with their start and end apart: 10 -> 51, of which waited for: 4 -> 24; matrix products, arithmetic and copies ran while one was open for 40% -> 22% of each run, Pallas kernels for 0% -> 17%
where the time goes in v1:
time: 609 us; the launch traced here: 600 us
  Pallas kernels  149 us (24%)
  waiting for transfers between devices  149 us (24%)
  starting transfers between devices  121 us (20%)
  other arithmetic  61 us (10%)
  matrix products  54.3 us (9%)
  local copies, waits for them, and re-layouts  43.4 us (7%)
  between operations  22.2 us (4%)
    ppermute x4, starting transfers between devices, tensor_sum(): return [total, lax.ppermute(total, 'tensor', LINE_PAIRS)]  68.8 us
    dot_general x16, matrix products, low_dot(): lax.dot_general(left.astype(bf16), right.astype(bf16), (dims, ((), ())),...  54.3 us
    ppermute x4, waiting for transfers between devices, tensor_sum(): total = pair + lax.ppermute(pair, 'tensor', LINE_ACROSS)  48.8 us
    pallas_call x2, Pallas kernels, feed_forward(): pl.pallas_call(kernel, grid=(blocks,), in_specs=[pl.BlockSpec(memory_spac...  48.5 us
    pallas_call x2, Pallas kernels, merge_in(): pl.pallas_call(kernel, grid=(depth // row_block,), in_specs=[pl.BlockSpec...  32.7 us
    ppermute x4, waiting for transfers between devices, tensor_sum(): return [total, lax.ppermute(total, 'tensor', LINE_PAIRS)]  30.5 us
    ppermute x4, waiting for transfers between devices, tensor_sum(): pair = keep + lax.ppermute(send, 'tensor', LINE_PAIRS)  27.6 us
    unnamed x187, local copies, waits for them, and re-layouts  20 us
  transfers between devices with their start and end apart: 51, of which 24 were waited for; matrix products, arithmetic and copies ran while one was open for 22% of the time, Pallas kernels for 17%

profile of v1, /device:TPU:0, one launch (start us, length us, event | category | flops | bytes accessed | tf_op | source)
XLA Modules:
  0.0 600.4 jit_solution(17028373169938672175)
XLA Ops:
  8.5 10.5 %copy.38.w_ref = bf16[2048,3,512]{2,1,0:T(4,128)(2,1)} copy(bf16[2048,3,512]{2,0,1:T(8,128)(2,1)} %param.31) | data formatting | bytes 12582912 | tf_op args[7]
  19.7 12.4 %merge_in.2 = (bf16[2048,1536]{1,0:T(8,128)(2,1)}, f32[1,1536]{1,0:T(1,128)}) custom-call(bf16[2048,3,512]{2,1,0:T(4,128)(2,1)} %copy.38.w_ref, f32[3,16,2048]{2,1,0:T(8,128)} %bitcast.197, f32[3,16,512]{2,1,0:T(8,128)} %b_ref.3), custom_call_target="tpu_custom_call" | custom-call | flops 301989888 | bytes 12582912 | tf_op jit(solution)/shard_map/merge_in/pallas_call | solution.py:551
  35.4 9.3 %project_in.1 = (bf16[512,2048]{1,0:T(8,128)(2,1)}, bf16[512,1536]{1,0:T(8,128)(2,1)}) custom-call(bf16[512,2048]{1,0:T(8,128)(2,1)} %bitcast.194, f32[1,2048]{1,0:T(1,128)} %bitcast.213, bf16[2048,1536]{1,0:T(8,128)(2,1)} %get-tuple-element.71.w_ref, f32[1,1536]{1,0:T(1,128)} %rsqrt_multiply_fusion.3.s_ref, f32[512,128]{1,0:T(8,128)} %get-tuple-element.221.c_ref, ...), custom_call_target="tpu_custom_call" | custom-call | flops 3221225472 | bytes 12058624 | tf_op jit(solution)/shard_map/project_in/pallas_call | solution.py:645
  46.5 3.0 collective-permute-start.2
  51.5 3.4 merge_out.2
  54.9 10.9 %merge_out.3 = (bf16[1408,2048]{1,0:T(8,128)(2,1)}, f32[1,2048]{1,0:T(1,128)}) custom-call(bf16[1408,2048]{1,0:T(8,128)(2,1)} %w_ref.5, f32[16,1408]{1,0:T(8,128)} %bitcast.201, f32[16,2048]{1,0:T(8,128)} %b_ref.5), custom_call_target="tpu_custom_call" | custom-call | flops 276824064 | bytes 11534336 | tf_op jit(solution)/shard_map/merge_out/pallas_call | solution.py:591
  81.2 3.1 slice_bitcast_fusion.2
  87.6 4.2 fusion.141
  109.8 3.9 collective-permute-done.10
  115.9 5.5 attend.2
  122.7 5.3 attend.3
  128.7 20.3 %merge_in.3 = (bf16[2048,2816]{1,0:T(8,128)(2,1)}, f32[1,2816]{1,0:T(1,128)}) custom-call(bf16[2048,2,1408]{2,1,0:T(2,128)(2,1)} %w_ref.6, f32[2,16,2048]{2,1,0:T(8,128)} %bitcast.198, f32[2,16,1408]{2,1,0:T(8,128)} %b_ref.6), custom_call_target="tpu_custom_call" | custom-call | flops 553648128 | bytes 23068672 | tf_op jit(solution)/shard_map/merge_in/pallas_call | solution.py:551
  150.6 3.9 collective-permute-start.6
  155.1 16.3 %collective-permute-done.6 = bf16[128,2048]{1,0:T(8,128)(2,1)S(1)} collective-permute-done((bf16[128,2048]{1,0:T(8,128)(2,1)S(1)}, bf16[128,2048]{1,0:T(8,128)(2,1)S(1)}, u32[]{:S(2)}, u32[]{:S(2)}) %collective-permute-start.6) | collective-permute-done | bytes 524320 | tf_op jit(solution)/shard_map/ppermute | solution.py:1035
  171.6 23.5 %collective-permute-start.7 = (bf16[128,2048]{1,0:T(8,128)(2,1)S(1)}, bf16[128,2048]{1,0:T(8,128)(2,1)S(1)}, u32[]{:S(2)}, u32[]{:S(2)}) collective-permute-start(bf16[128,2048]{1,0:T(8,128)(2,1)S(1)} %add.167.refs_1_.refs_3_), channel_id=1, source_target_pairs={{0,1},{1,0},{2,3},{3,2},{4,5},{5,4},{6,7},{7,6},{8,9},{9,8},{10,11... | collective-permute-start | bytes 1572872 | tf_op jit(solution)/shard_map/ppermute | solution.py:1036
  195.1 24.0 %feed_forward.3 = (f32[256,2048]{1,0:T(8,128)}, bf16[256,2048]{1,0:T(8,128)(2,1)}, bf16[256,2048]{1,0:T(8,128)(2,1)}, bf16[256,1408]{1,0:T(8,128)(2,1)}, bf16[25...) custom-call(s32[2]{0:T(128)} %pad_add_fusion.1.refs_0_, ...), custom_call_target="tpu_custom_call" | custom-call | flops 8858370048 | bytes 25690112 | tf_op jit(solution)/shard_map/feed_forward/pallas_call | solution.py:814
  219.9 24.5 %feed_forward.2 = (f32[256,2048]{1,0:T(8,128)}, bf16[256,2048]{1,0:T(8,128)(2,1)}, bf16[256,2048]{1,0:T(8,128)(2,1)}, bf16[256,1408]{1,0:T(8,128)(2,1)}, bf16[25...) custom-call(s32[2]{0:T(128)} %pad_add_fusion.refs_0_, ...), custom_call_target="tpu_custom_call" | custom-call | flops 8858370048 | bytes 25690112 | tf_op jit(solution)/shard_map/feed_forward/pallas_call | solution.py:814
  250.8 7.2 %fusion = f32[32,2816]{1,0:T(8,128)} fusion(bf16[32,2048]{1,0:T(8,128)(2,1)S(1)} %bitcast.199, bf16[2048,2816]{1,0:T(8,128)(2,1)} %get-tuple-element.81.refs_8_.refs_9_.refs_7_, f32[2816]{0:T(1024)S(1)} %fusion.87), kind=kOutput, calls=%fused_computation.2 | convolution fusion | flops 369188864 | bytes 12037120 | tf_op jit(solution)/shard_map/dot_general | solution.py:1086
  260.3 4.1 fusion.45
  264.4 20.8 %collective-permute-done.15 = bf16[128,2048]{1,0:T(8,128)(2,1)S(1)} collective-permute-done((bf16[128,2048]{1,0:T(8,128)(2,1)S(1)}, bf16[128,2048]{1,0:T(8,128)(2,1)S(1)}, u32[]{:S(2)}, u32[]{:S(2)}) %collective-permute-start.15) | collective-permute-done | bytes 524320 | tf_op jit(solution)/shard_map/ppermute | solution.py:1035
  285.4 27.5 %collective-permute-start.16 = (bf16[128,2048]{1,0:T(8,128)(2,1)S(1)}, bf16[128,2048]{1,0:T(8,128)(2,1)S(1)}, u32[]{:S(2)}, u32[]{:S(2)}) collective-permute-start(bf16[128,2048]{1,0:T(8,128)(2,1)S(1)} %add.174.refs_1_), channel_id=1, source_target_pairs={{0,1},{1,0},{2,3},{3,2},{4,5},{5,4},{6,7},{7,6},{8,9},{9,8},{10,11... | collective-permute-start | bytes 1572872 | tf_op jit(solution)/shard_map/ppermute | solution.py:1036
  312.9 4.2 fusion.9
  317.1 4.4 convolution_subtract_fusion
  321.5 20.5 %collective-permute-done.16.refs_2_ = bf16[128,2048]{1,0:T(8,128)(2,1)S(1)} collective-permute-done((bf16[128,2048]{1,0:T(8,128)(2,1)S(1)}, bf16[128,2048]{1,0:T(8,128)(2,1)S(1)}, u32[]{:S(2)}, u32[]{:S(2)}) %collective-permute-start.16) | collective-permute-done | bytes 524320 | tf_op jit(solution)/shard_map/ppermute | solution.py:1036
  342.8 9.3 %attend_back.2 = (f32[256,2048]{1,0:T(8,128)}, bf16[256,2048]{1,0:T(8,128)(2,1)}, f32[1,2048]{1,0:T(1,128)}, f32[256,1536]{1,0:T(8,128)}, bf16[128,1024]{1,0:T(8,128)(2,1)}) custom-call(s32[2]{0:T(128)} %pad_add_fusion.refs_0_, bf16[128,2048]{1,0:T(8,128)(2,1)} %copy-done.11, bf16[128,2048]{1,0:T(8,128)(2,1)} %copy-done.36, bf16[128,2048]{1,0:T(8,128)(2,1)} %copy-done.10, ...), custom_call_target="tpu_custom_call" | custom-call | flops 1040187392 | bytes 12845056 | tf_op jit(solution)/shard_map/attend_back/pallas_call | solution.py:943
  355.7 10.0 %collective-permute-done.18 = bf16[128,1024]{1,0:T(8,128)(2,1)S(1)} collective-permute-done((bf16[128,1024]{1,0:T(8,128)(2,1)}, bf16[128,1024]{1,0:T(8,128)(2,1)S(1)}, u32[]{:S(2)}, u32[]{:S(2)}) %collective-permute-start.18) | collective-permute-done | bytes 262176 | tf_op jit(solution)/shard_map/ppermute | solution.py:1066
  370.4 7.7 %project_back.2 = (bf16[256,1536]{1,0:T(8,128)(2,1)}, f32[1,1536]{1,0:T(1,128)}, bf16[128,2048]{1,0:T(8,128)(2,1)}, bf16[128,2048]{1,0:T(8,128)(2,1)}) custom-call(s32[1]{0:T(128)} %bitcast.1.i_ref, f32[256,1536]{1,0:T(8,128)} %get-tuple-element.92.d_ref, bf16[128,1024]{1,0:T(8,128)(2,1)} %select_select_fusion.6.r_ref, ...), custom_call_target="tpu_custom_call" | custom-call | flops 1610612736 | bytes 11272192 | tf_op jit(solution)/shard_map/project_back/pallas_call | solution.py:993
  383.2 27.6 %collective-permute-done.21 = bf16[128,2048]{1,0:T(8,128)(2,1)} collective-permute-done((bf16[128,2048]{1,0:T(8,128)(2,1)}, bf16[128,2048]{1,0:T(8,128)(2,1)}, u32[]{:S(2)}, u32[]{:S(2)}) %collective-permute-start.21) | collective-permute-done | bytes 524320 | tf_op jit(solution)/shard_map/ppermute | solution.py:1034
  417.4 8.9 %attend_back.3 = (f32[256,2048]{1,0:T(8,128)}, bf16[256,2048]{1,0:T(8,128)(2,1)}, f32[1,2048]{1,0:T(1,128)}, f32[256,1536]{1,0:T(8,128)}, bf16[128,1024]{1,0:T(8,128)(2,1)}) custom-call(s32[2]{0:T(128)} %pad_add_fusion.1.refs_0_, bf16[256,2048]{1,0:T(8,128)(2,1)} %get-tuple-element.148.refs_1_, ...), custom_call_target="tpu_custom_call" | custom-call | flops 1040187392 | bytes 12845056 | tf_op jit(solution)/shard_map/attend_back/pallas_call | solution.py:943
  431.9 8.0 %collective-permute-start.23 = (bf16[128,2048]{1,0:T(8,128)(2,1)}, bf16[128,2048]{1,0:T(8,128)(2,1)}, u32[]{:S(2)}, u32[]{:S(2)}) collective-permute-start(bf16[128,2048]{1,0:T(8,128)(2,1)} %add.177), channel_id=1, source_target_pairs={{0,1},{1,0},{2,3},{3,2},{4,5},{5,4},{6,7},{7,6},{8,9},{9,8},{10,11... | collective-permute-start | bytes 1572872 | tf_op jit(solution)/shard_map/ppermute | solution.py:1036
  443.0 4.9 fusion.75
  447.9 3.6 fusion.15
  451.5 3.6 fusion.16
  455.8 3.4 concatenate.152
  460.0 4.4 fusion.33
  467.9 3.2 fusion.14
  476.9 2.6 fusion.32
  480.7 2.6 collective-permute-start.45
  497.1 7.5 %project_back.3 = (bf16[256,1536]{1,0:T(8,128)(2,1)}, f32[1,1536]{1,0:T(1,128)}, bf16[128,2048]{1,0:T(8,128)(2,1)}, bf16[128,2048]{1,0:T(8,128)(2,1)}) custom-call(s32[1]{0:T(128)} %bitcast.1.i_ref, f32[256,1536]{1,0:T(8,128)} %get-tuple-element.98.d_ref, bf16[128,1024]{1,0:T(8,128)(2,1)} %select_select_fusion.4.r_ref, ...), custom_call_target="tpu_custom_call" | custom-call | flops 1610612736 | bytes 11272192 | tf_op jit(solution)/shard_map/project_back/pallas_call | solution.py:993
  508.6 2.7 fusion.55
  511.3 3.1 fusion.7
  514.4 3.0 convolution_subtract_fusion.1
  519.8 4.3 collective-permute-done.32
  525.7 2.6 collective-permute-done.33
  535.3 2.8 collective-permute-done.35
  553.6 11.6 %collective-permute-done.29 = bf16[128,2048]{1,0:T(8,128)(2,1)S(1)} collective-permute-done((bf16[128,2048]{1,0:T(8,128)(2,1)S(1)}, bf16[128,2048]{1,0:T(8,128)(2,1)S(1)}, u32[]{:S(2)}, u32[]{:S(2)}) %collective-permute-start.29) | collective-permute-done | bytes 524320 | tf_op jit(solution)/shard_map/ppermute | solution.py:1035
  565.4 9.8 %collective-permute-start.30 = (bf16[128,2048]{1,0:T(8,128)(2,1)S(1)}, bf16[128,2048]{1,0:T(8,128)(2,1)S(1)}, u32[]{:S(2)}, u32[]{:S(2)}) collective-permute-start(bf16[128,2048]{1,0:T(8,128)(2,1)S(1)} %add.181), channel_id=1, source_target_pairs={{0,1},{1,0},{2,3},{3,2},{4,5},{5,4},{6,7},{7,6},{8,9},{9,8},{10,11... | collective-permute-start | bytes 1572872 | tf_op jit(solution)/shard_map/ppermute | solution.py:1036
  577.1 10.0 %collective-permute-done.30 = bf16[128,2048]{1,0:T(8,128)(2,1)S(1)} collective-permute-done((bf16[128,2048]{1,0:T(8,128)(2,1)S(1)}, bf16[128,2048]{1,0:T(8,128)(2,1)S(1)}, u32[]{:S(2)}, u32[]{:S(2)}) %collective-permute-start.30) | collective-permute-done | bytes 524320 | tf_op jit(solution)/shard_map/ppermute | solution.py:1036
  (406 shorter events, 148.4 us)
Async XLA Ops:
  7.2 187.9 %all-reduce.17.cloned.1.call-start = ((), (), s32[]{:S(2)}) async-start(), calls=%async_computation | async-start | bytes 2097152 | tf_op jit(solution)/shard_map/psum | solution.py:1032
  46.5 54.2 %collective-permute-start.2 = (bf16[144,1024]{1,0:T(8,128)(2,1)}, bf16[144,1024]{1,0:T(8,128)(2,1)}, u32[]{:S(2)}, u32[]{:S(2)}) collective-permute-start(bf16[144,1024]{1,0:T(8,128)(2,1)} %fusion.40), channel_id=1, source_target_pairs={{0,16},{4,20},{8,24},{12,28},{16,0},{20,4},{24,8},{28,12},{1,17},{... | collective-permute-start | bytes 884744 | tf_op jit(solution)/shard_map/ppermute | solution.py:1066
  49.5 51.8 %collective-permute-start.3 = (bf16[144,1024]{1,0:T(8,128)(2,1)}, bf16[144,1024]{1,0:T(8,128)(2,1)}, u32[]{:S(2)}, u32[]{:S(2)}) collective-permute-start(bf16[144,1024]{1,0:T(8,128)(2,1)} %fusion.40), channel_id=1, source_target_pairs={{0,24},{4,28},{8,16},{12,20},{16,8},{20,12},{24,0},{28,4},{1,25},{... | collective-permute-start | bytes 884744 | tf_op jit(solution)/shard_map/ppermute | solution.py:1066
  50.9 52.8 %collective-permute-start.1 = (bf16[144,1024]{1,0:T(8,128)(2,1)}, bf16[144,1024]{1,0:T(8,128)(2,1)}, u32[]{:S(2)}, u32[]{:S(2)}) collective-permute-start(bf16[144,1024]{1,0:T(8,128)(2,1)} %fusion.40), channel_id=1, source_target_pairs={{0,8},{4,12},{8,0},{12,4},{16,24},{20,28},{24,16},{28,20},{1,9},{5... | collective-permute-start | bytes 884744 | tf_op jit(solution)/shard_map/ppermute | solution.py:1066
  51.5 42.8 %collective-permute-start = (s32[2]{0:T(128)}, s32[2]{0:T(128)}, u32[]{:S(2)}, u32[]{:S(2)}) collective-permute-start(s32[2]{0:T(128)} %fusion.177), channel_id=1, source_target_pairs={{0,4},{4,0},{8,12},{12,8},{16,20},{20,16},{24,28},{28,24},{1,5},{5... | collective-permute-start | bytes 32 | tf_op jit(solution)/shard_map/ppermute | solution.py:1166
  67.3 31.1 %collective-permute-start.8 = (f32[2,2048]{1,0:T(2,128)}, f32[2,2048]{1,0:T(2,128)}, u32[]{:S(2)}, u32[]{:S(2)}) collective-permute-start(f32[2,2048]{1,0:T(2,128)} %pad_maximum_fusion.12), channel_id=1, source_target_pairs={{0,1},{1,0},{2,3},{3,2},{4,5},{5,4},{6,7},{7,6},{8,9},{9,8},{10,11... | collective-permute-start | bytes 49160 | tf_op jit(solution)/shard_map/ppermute | solution.py:1040
  94.3 15.5 %collective-permute-start.11 = (bf16[144,1024]{1,0:T(8,128)(2,1)S(1)}, bf16[144,1024]{1,0:T(8,128)(2,1)S(1)}, u32[]{:S(2)}, u32[]{:S(2)}) collective-permute-start(bf16[144,1024]{1,0:T(8,128)(2,1)S(1)} %fusion.41), channel_id=1, source_target_pairs={{0,16},{4,20},{8,24},{12,28},{16,0},{20,4},{24,8},{28,12},{1,17},{... | collective-permute-start | bytes 884744 | tf_op jit(solution)/shard_map/ppermute | solution.py:1066
  98.5 11.3 %collective-permute-start.12 = (bf16[144,1024]{1,0:T(8,128)(2,1)S(1)}, bf16[144,1024]{1,0:T(8,128)(2,1)S(1)}, u32[]{:S(2)}, u32[]{:S(2)}) collective-permute-start(bf16[144,1024]{1,0:T(8,128)(2,1)S(1)} %fusion.41), channel_id=1, source_target_pairs={{0,24},{4,28},{8,16},{12,20},{16,8},{20,12},{24,0},{28,4},{1,25},{... | collective-permute-start | bytes 884744 | tf_op jit(solution)/shard_map/ppermute | solution.py:1066
  100.8 12.9 %collective-permute-start.10 = (bf16[144,1024]{1,0:T(8,128)(2,1)S(1)}, bf16[144,1024]{1,0:T(8,128)(2,1)S(1)}, u32[]{:S(2)}, u32[]{:S(2)}) collective-permute-start(bf16[144,1024]{1,0:T(8,128)(2,1)S(1)} %fusion.41), channel_id=1, source_target_pairs={{0,8},{4,12},{8,0},{12,4},{16,24},{20,28},{24,16},{28,20},{1,9},{5... | collective-permute-start | bytes 884744 | tf_op jit(solution)/shard_map/ppermute | solution.py:1066
  101.3 5.5 collective-permute-start.9
  104.9 9.0 %collective-permute-start.4 = (bf16[144,1024]{1,0:T(8,128)(2,1)S(1)}, bf16[144,1024]{1,0:T(8,128)(2,1)S(1)}, u32[]{:S(2)}, u32[]{:S(2)}) collective-permute-start(bf16[144,1024]{1,0:T(8,128)(2,1)S(1)} %select_select_fusion.3), channel_id=1, source_target_pairs={{0,4},{4,0},{8,12},{12,8},{16,20},{20,16},{24,28},{28,24},{1,5},{5... | collective-permute-start | bytes 884744 | tf_op jit(solution)/shard_map/ppermute | solution.py:1073
  113.9 7.8 %collective-permute-start.13 = (bf16[144,1024]{1,0:T(8,128)(2,1)S(1)}, bf16[144,1024]{1,0:T(8,128)(2,1)S(1)}, u32[]{:S(2)}, u32[]{:S(2)}) collective-permute-start(bf16[144,1024]{1,0:T(8,128)(2,1)S(1)} %select_select_fusion.1), channel_id=1, source_target_pairs={{0,4},{4,0},{8,12},{12,8},{16,20},{20,16},{24,28},{28,24},{1,5},{5... | collective-permute-start | bytes 884744 | tf_op jit(solution)/shard_map/ppermute | solution.py:1073
  121.4 29.1 %collective-permute-start.5 = (bf16[128,2048]{1,0:T(8,128)(2,1)}, bf16[128,2048]{1,0:T(8,128)(2,1)S(1)}, u32[]{:S(2)}, u32[]{:S(2)}) collective-permute-start(bf16[128,2048]{1,0:T(8,128)(2,1)} %get-tuple-element.76), channel_id=1, source_target_pairs={{0,1},{1,0},{2,3},{3,2},{4,5},{5,4},{6,7},{7,6},{8,9},{9,8},{10,11... | collective-permute-start | bytes 1572872 | tf_op jit(solution)/shard_map/ppermute | solution.py:1034
  128.0 289.3 %all-reduce.19.cloned.1.call-start = ((), (), s32[]{:S(2)}) async-start(), calls=%async_computation.1 | async-start | bytes 6291456 | tf_op jit(solution)/shard_map/psum | solution.py:1032
  150.6 20.9 %collective-permute-start.6 = (bf16[128,2048]{1,0:T(8,128)(2,1)S(1)}, bf16[128,2048]{1,0:T(8,128)(2,1)S(1)}, u32[]{:S(2)}, u32[]{:S(2)}) collective-permute-start(bf16[128,2048]{1,0:T(8,128)(2,1)S(1)} %add.166), channel_id=1, source_target_pairs={{0,3},{3,0},{1,2},{2,1},{4,7},{7,4},{5,6},{6,5},{8,11},{11,8},{9,1... | collective-permute-start | bytes 1572872 | tf_op jit(solution)/shard_map/ppermute | solution.py:1035
  171.6 47.5 %collective-permute-start.7 = (bf16[128,2048]{1,0:T(8,128)(2,1)S(1)}, bf16[128,2048]{1,0:T(8,128)(2,1)S(1)}, u32[]{:S(2)}, u32[]{:S(2)}) collective-permute-start(bf16[128,2048]{1,0:T(8,128)(2,1)S(1)} %add.167.refs_1_.refs_3_), channel_id=1, source_target_pairs={{0,1},{1,0},{2,3},{3,2},{4,5},{5,4},{6,7},{7,6},{8,9},{9,8},{10,11... | collective-permute-start | bytes 1572872 | tf_op jit(solution)/shard_map/ppermute | solution.py:1036
  244.4 13.6 %collective-permute-start.14 = (bf16[128,2048]{1,0:T(8,128)(2,1)}, bf16[128,2048]{1,0:T(8,128)(2,1)S(1)}, u32[]{:S(2)}, u32[]{:S(2)}) collective-permute-start(bf16[128,2048]{1,0:T(8,128)(2,1)} %get-tuple-element.90), channel_id=1, source_target_pairs={{0,1},{1,0},{2,3},{3,2},{4,5},{5,4},{6,7},{7,6},{8,9},{9,8},{10,11... | collective-permute-start | bytes 1572872 | tf_op jit(solution)/shard_map/ppermute | solution.py:1034
  245.9 134.8 %collective-permute-start.39 = (f32[1,2048]{1,0:T(1,128)}, f32[1,2048]{1,0:T(1,128)}, u32[]{:S(2)}, u32[]{:S(2)}) collective-permute-start(f32[1,2048]{1,0:T(1,128)} %add.191), channel_id=1, source_target_pairs={{0,1},{1,0},{2,3},{3,2},{4,5},{5,4},{6,7},{7,6},{8,9},{9,8},{10,11... | collective-permute-start | bytes 24584 | tf_op jit(solution)/shard_map/ppermute | solution.py:1040
  258.2 27.1 %collective-permute-start.15 = (bf16[128,2048]{1,0:T(8,128)(2,1)S(1)}, bf16[128,2048]{1,0:T(8,128)(2,1)S(1)}, u32[]{:S(2)}, u32[]{:S(2)}) collective-permute-start(bf16[128,2048]{1,0:T(8,128)(2,1)S(1)} %add.173), channel_id=1, source_target_pairs={{0,3},{3,0},{1,2},{2,1},{4,7},{7,4},{5,6},{6,5},{8,11},{11,8},{9,1... | collective-permute-start | bytes 1572872 | tf_op jit(solution)/shard_map/ppermute | solution.py:1035
  285.4 56.6 %collective-permute-start.16 = (bf16[128,2048]{1,0:T(8,128)(2,1)S(1)}, bf16[128,2048]{1,0:T(8,128)(2,1)S(1)}, u32[]{:S(2)}, u32[]{:S(2)}) collective-permute-start(bf16[128,2048]{1,0:T(8,128)(2,1)S(1)} %add.174.refs_1_), channel_id=1, source_target_pairs={{0,1},{1,0},{2,3},{3,2},{4,5},{5,4},{6,7},{7,6},{8,9},{9,8},{10,11... | collective-permute-start | bytes 1572872 | tf_op jit(solution)/shard_map/ppermute | solution.py:1036
  352.1 13.6 %collective-permute-start.18 = (bf16[128,1024]{1,0:T(8,128)(2,1)}, bf16[128,1024]{1,0:T(8,128)(2,1)S(1)}, u32[]{:S(2)}, u32[]{:S(2)}) collective-permute-start(bf16[128,1024]{1,0:T(8,128)(2,1)} %get-tuple-element.93), channel_id=1, source_target_pairs={{0,16},{4,20},{8,24},{12,28},{16,0},{20,4},{24,8},{28,12},{1,17},{... | collective-permute-start | bytes 786440 | tf_op jit(solution)/shard_map/ppermute | solution.py:1066
  353.3 12.4 %collective-permute-start.19 = (bf16[128,1024]{1,0:T(8,128)(2,1)}, bf16[128,1024]{1,0:T(8,128)(2,1)S(1)}, u32[]{:S(2)}, u32[]{:S(2)}) collective-permute-start(bf16[128,1024]{1,0:T(8,128)(2,1)} %get-tuple-element.93), channel_id=1, source_target_pairs={{0,24},{4,28},{8,16},{12,20},{16,8},{20,12},{24,0},{28,4},{1,25},{... | collective-permute-start | bytes 786440 | tf_op jit(solution)/shard_map/ppermute | solution.py:1066
  354.9 12.0 %collective-permute-start.17 = (bf16[128,1024]{1,0:T(8,128)(2,1)}, bf16[128,1024]{1,0:T(8,128)(2,1)S(1)}, u32[]{:S(2)}, u32[]{:S(2)}) collective-permute-start(bf16[128,1024]{1,0:T(8,128)(2,1)} %get-tuple-element.93), channel_id=1, source_target_pairs={{0,8},{4,12},{8,0},{12,4},{16,24},{20,28},{24,16},{28,20},{1,9},{5... | collective-permute-start | bytes 786440 | tf_op jit(solution)/shard_map/ppermute | solution.py:1066
  378.1 32.7 %collective-permute-start.21 = (bf16[128,2048]{1,0:T(8,128)(2,1)}, bf16[128,2048]{1,0:T(8,128)(2,1)}, u32[]{:S(2)}, u32[]{:S(2)}) collective-permute-start(bf16[128,2048]{1,0:T(8,128)(2,1)} %get-tuple-element.95), channel_id=1, source_target_pairs={{0,1},{1,0},{2,3},{3,2},{4,5},{5,4},{6,7},{7,6},{8,9},{9,8},{10,11... | collective-permute-start | bytes 1572872 | tf_op jit(solution)/shard_map/ppermute | solution.py:1034
  381.4 58.5 %collective-permute-start.40 = (f32[1,2048]{1,0:T(1,128)S(1)}, f32[1,2048]{1,0:T(1,128)S(1)}, u32[]{:S(2)}, u32[]{:S(2)}) collective-permute-start(f32[1,2048]{1,0:T(1,128)S(1)} %add.192), channel_id=1, source_target_pairs={{0,3},{3,0},{1,2},{2,1},{4,7},{7,4},{5,6},{6,5},{8,11},{11,8},{9,1... | collective-permute-start | bytes 24584 | tf_op jit(solution)/shard_map/ppermute | solution.py:1041
  412.9 16.9 %collective-permute-start.22 = (bf16[128,2048]{1,0:T(8,128)(2,1)}, bf16[128,2048]{1,0:T(8,128)(2,1)}, u32[]{:S(2)}, u32[]{:S(2)}) collective-permute-start(bf16[128,2048]{1,0:T(8,128)(2,1)} %add.176), channel_id=1, source_target_pairs={{0,3},{3,0},{1,2},{2,1},{4,7},{7,4},{5,6},{6,5},{8,11},{11,8},{9,1... | collective-permute-start | bytes 1572872 | tf_op jit(solution)/shard_map/ppermute | solution.py:1035
  426.3 61.7 %collective-permute-start.25 = (bf16[128,1024]{1,0:T(8,128)(2,1)}, bf16[128,1024]{1,0:T(8,128)(2,1)}, u32[]{:S(2)}, u32[]{:S(2)}) collective-permute-start(bf16[128,1024]{1,0:T(8,128)(2,1)} %get-tuple-element.99), channel_id=1, source_target_pairs={{0,16},{4,20},{8,24},{12,28},{16,0},{20,4},{24,8},{28,12},{1,17},{... | collective-permute-start | bytes 786440 | tf_op jit(solution)/shard_map/ppermute | solution.py:1066
  427.8 60.2 %collective-permute-start.26 = (bf16[128,1024]{1,0:T(8,128)(2,1)}, bf16[128,1024]{1,0:T(8,128)(2,1)}, u32[]{:S(2)}, u32[]{:S(2)}) collective-permute-start(bf16[128,1024]{1,0:T(8,128)(2,1)} %get-tuple-element.99), channel_id=1, source_target_pairs={{0,24},{4,28},{8,16},{12,20},{16,8},{20,12},{24,0},{28,4},{1,25},{... | collective-permute-start | bytes 786440 | tf_op jit(solution)/shard_map/ppermute | solution.py:1066
  429.2 58.8 %collective-permute-start.24 = (bf16[128,1024]{1,0:T(8,128)(2,1)}, bf16[128,1024]{1,0:T(8,128)(2,1)}, u32[]{:S(2)}, u32[]{:S(2)}) collective-permute-start(bf16[128,1024]{1,0:T(8,128)(2,1)} %get-tuple-element.99), channel_id=1, source_target_pairs={{0,8},{4,12},{8,0},{12,4},{16,24},{20,28},{24,16},{28,20},{1,9},{5... | collective-permute-start | bytes 786440 | tf_op jit(solution)/shard_map/ppermute | solution.py:1066
  431.9 60.9 %collective-permute-start.23 = (bf16[128,2048]{1,0:T(8,128)(2,1)}, bf16[128,2048]{1,0:T(8,128)(2,1)}, u32[]{:S(2)}, u32[]{:S(2)}) collective-permute-start(bf16[128,2048]{1,0:T(8,128)(2,1)} %add.177), channel_id=1, source_target_pairs={{0,1},{1,0},{2,3},{3,2},{4,5},{5,4},{6,7},{7,6},{8,9},{9,8},{10,11... | collective-permute-start | bytes 1572872 | tf_op jit(solution)/shard_map/ppermute | solution.py:1036
  459.3 6.2 %collective-permute-start.41 = (bf16[112,1024]{1,0:T(8,128)(2,1)S(1)}, bf16[112,1024]{1,0:T(8,128)(2,1)S(1)}, u32[]{:S(2)}, u32[]{:S(2)}) collective-permute-start(bf16[112,1024]{1,0:T(8,128)(2,1)S(1)} %broadcast_select_fusion.6), channel_id=1, source_target_pairs={{0,4},{4,0},{8,12},{12,8},{16,20},{20,16},{24,28},{28,24},{1,5},{5... | collective-permute-start | bytes 688136 | tf_op jit(solution)/shard_map/ppermute | solution.py:1053
  466.3 5.3 collective-permute-start.42
  472.5 4.2 collective-permute-start.43
  480.7 5.6 collective-permute-start.45
  486.4 4.2 collective-permute-start.46
  489.3 5.8 collective-permute-start.27
  491.3 26.4 %collective-permute-start.47 = (bf16[112,512]{1,0:T(8,128)(2,1)}, bf16[112,512]{1,0:T(8,128)(2,1)}, u32[]{:S(2)}, u32[]{:S(2)}) collective-permute-start(bf16[112,512]{1,0:T(8,128)(2,1)} %pad_maximum_fusion.6), channel_id=1, source_target_pairs={{0,8},{4,12},{8,0},{12,4},{16,24},{20,28},{24,16},{28,20},{1,9},{5... | collective-permute-start | bytes 344072 | tf_op jit(solution)/shard_map/ppermute | solution.py:1057
  504.6 43.2 %collective-permute-start.28 = (bf16[128,2048]{1,0:T(8,128)(2,1)}, bf16[128,2048]{1,0:T(8,128)(2,1)}, u32[]{:S(2)}, u32[]{:S(2)}) collective-permute-start(bf16[128,2048]{1,0:T(8,128)(2,1)} %get-tuple-element.101), channel_id=1, source_target_pairs={{0,1},{1,0},{2,3},{3,2},{4,5},{5,4},{6,7},{7,6},{8,9},{9,8},{10,11... | collective-permute-start | bytes 1572872 | tf_op jit(solution)/shard_map/ppermute | solution.py:1034
  519.2 4.9 collective-permute-start.32
  519.7 5.9 collective-permute-start.48
  524.2 4.2 collective-permute-start.33
  528.4 4.0 collective-permute-start.34
  532.3 5.8 collective-permute-start.35
  538.1 4.2 collective-permute-start.36
  542.3 4.7 collective-permute-start.37
  547.1 4.3 collective-permute-start.38
  549.0 16.3 %collective-permute-start.29 = (bf16[128,2048]{1,0:T(8,128)(2,1)S(1)}, bf16[128,2048]{1,0:T(8,128)(2,1)S(1)}, u32[]{:S(2)}, u32[]{:S(2)}) collective-permute-start(bf16[128,2048]{1,0:T(8,128)(2,1)S(1)} %add.180), channel_id=1, source_target_pairs={{0,3},{3,0},{1,2},{2,1},{4,7},{7,4},{5,6},{6,5},{8,11},{11,8},{9,1... | collective-permute-start | bytes 1572872 | tf_op jit(solution)/shard_map/ppermute | solution.py:1035
  565.4 21.7 %collective-permute-start.30 = (bf16[128,2048]{1,0:T(8,128)(2,1)S(1)}, bf16[128,2048]{1,0:T(8,128)(2,1)S(1)}, u32[]{:S(2)}, u32[]{:S(2)}) collective-permute-start(bf16[128,2048]{1,0:T(8,128)(2,1)S(1)} %add.181), channel_id=1, source_target_pairs={{0,1},{1,0},{2,3},{3,2},{4,5},{5,4},{6,7},{7,6},{8,9},{9,8},{10,11... | collective-permute-start | bytes 1572872 | tf_op jit(solution)/shard_map/ppermute | solution.py:1036
  (92 other events, 1189.7 us)
Sparse Core Ops, SparseCore 0:
  128.1 64.5 all-reduce.16
  250.8 158.0 all-reduce.18
